TPU v7x, 32 devices: a whole 2x2x4 slice. The times are simulated.
32 devices in a mesh: groups: 2 (over y), tgt: 4 (over z), src: 2 (over x), sub: 2 (over core).
Axes of the slice: x: 2, y: 2, z: 4, core: 2. Of those that a mesh axis runs over, the one named last changes fastest.
Arguments:
- src_words: int32 [2048], P(('groups', 'tgt', 'src', 'sub')), parts along dimension 0, may hold values from 0 to 12543, as said below
- tgt_words: int32 [2048], P(('groups', 'tgt', 'src', 'sub')), parts along dimension 0, may hold values from 0 to 12543, as said below
- src_vocab: bfloat16 [25088, 300], P(('groups', 'tgt', 'src', 'sub')), parts along dimension 0, may hold values from -3 to 3
- tgt_vocab: bfloat16 [25088, 300], P(('groups', 'tgt', 'src', 'sub')), parts along dimension 0, may hold values from -3 to 3
- mapping: float32 [600, 300], P('groups'), parts along dimension 0, may hold values from -1 to 2
Outputs:
- source_potential: float32 [2048], P(('groups', 'tgt', 'src', 'sub')), parts along dimension 0
- target_potential: float32 [2048], P(('groups', 'tgt', 'src', 'sub')), parts along dimension 0
- rotation: float32 [600, 300], P('groups'), parts along dimension 0
There are 2 independent parts, one for each index of `groups`. A program takes and returns all parts, laid end to end along the dimension named above; each array names one. Nothing has to cross between parts.
Inputs may be any that keep to these rules, and one draw needn't show every extreme that they name: `src_words`: position p names a word of rows q * 784 to (q + 1) * 784 - 1 of the source vocabulary, q = p // 64; in each such block of 64 positions the first names the block's first word and the second its last word. `tgt_words`: position p names a word of rows q * 784 to (q + 1) * 784 - 1 of the target vocabulary, q = p // 64; in each such block of 64 positions the first names the block's first word and the second its last word.
All inputs are finite; a program needn't handle non-finite values.
Results may differ from a plain program's by a relative error of at most 0.0077.
Values may be sent and summed in bfloat16 or wider, within the bound.
No kernel may reach another device: no remote copies, remote signals or barrier semaphores. Data moves between devices by JAX's collectives and lax.ppermute only.
A program may use at most 64 MiB of HBM per device.

v0:
```python
import math

import jax
import jax.numpy as jnp
from jax import lax
from jax.sharding import PartitionSpec as P

ITERS = 4
POLAR_STEPS = 8


entropy_scale = 0.05


def row_log_total(logits):
    peak = lax.pmax(jnp.max(logits, axis=1), "tgt")
    mass = lax.psum(jnp.sum(jnp.exp(logits - peak[:, None]), axis=1), "tgt")
    return peak + jnp.log(mass)


def col_log_total(logits):
    peak = lax.pmax(jnp.max(logits, axis=0), ("src", "sub"))
    mass = lax.psum(jnp.sum(jnp.exp(logits - peak[None, :]), axis=0), ("src", "sub"))
    return peak + jnp.log(mass)


def local(src_words, tgt_words, src_vocab, tgt_vocab, mapping):
    highest = lax.Precision.HIGHEST
    vocab_rows = src_vocab.shape[0]
    place = lax.axis_index(("tgt", "src", "sub"))
    own_source = jnp.take(src_vocab, src_words - place * vocab_rows, axis=0)
    own_target = jnp.take(tgt_vocab, tgt_words - place * vocab_rows, axis=0)
    own_projected = jnp.dot(own_source.astype(jnp.float32), mapping, precision=highest).astype(
        jnp.bfloat16
    )
    projected = lax.all_gather(own_projected, "tgt", axis=0, tiled=True)
    target_tile = lax.all_gather(own_target, ("src", "sub"), axis=0, tiled=True)
    scores = jnp.einsum("rd,cd->rc", projected, target_tile, preferred_element_type=jnp.float32)
    local_rows = own_source.shape[0]
    width = own_source.shape[1]
    total = local_rows * lax.axis_size(("tgt", "src", "sub"))
    log_mass = entropy_scale * math.log(1.0 / total)
    log_total = math.log(total)
    col_pot = jnp.zeros((scores.shape[1],), jnp.float32)
    row_pot = jnp.zeros((scores.shape[0],), jnp.float32)
    for step in range(ITERS):
        row_pot = log_mass - entropy_scale * row_log_total(
            (col_pot[None, :] + scores) / entropy_scale
        )
        col_pot = log_mass - entropy_scale * col_log_total(
            (row_pot[:, None] + scores) / entropy_scale
        )
    plan = jnp.exp(
        (row_pot[:, None] + col_pot[None, :] + scores) / entropy_scale + log_total
    ).astype(jnp.bfloat16)
    own_bary = lax.psum_scatter(
        jnp.dot(plan, target_tile, preferred_element_type=jnp.float32),
        "tgt",
        scatter_dimension=0,
        tiled=True,
    )
    partial_cov = jnp.einsum(
        "rd,re->de", own_source.astype(jnp.float32), own_bary, precision=highest
    )
    cov = lax.psum(partial_cov, ("tgt", "src", "sub"))
    polar = cov / jnp.sqrt(jnp.sum(cov * cov))
    for step in range(POLAR_STEPS):
        square = jnp.dot(polar, polar.T, precision=highest)
        polar = 1.5 * polar - 0.5 * jnp.dot(square, polar, precision=highest)
    rotation = math.sqrt(width) * polar
    source_potential = lax.dynamic_slice_in_dim(
        row_pot, lax.axis_index("tgt") * local_rows, local_rows, 0
    )
    target_potential = lax.dynamic_slice_in_dim(
        col_pot, lax.axis_index(("src", "sub")) * local_rows, local_rows, 0
    )
    return (source_potential, target_potential, rotation)


def solution(mesh):
    placed = (
        P(("groups", "tgt", "src", "sub")),
        P(("groups", "tgt", "src", "sub")),
        P(("groups", "tgt", "src", "sub"), None),
        P(("groups", "tgt", "src", "sub"), None),
        P("groups", None),
    )
    return jax.shard_map(
        local,
        mesh=mesh,
        in_specs=placed,
        out_specs=(
            P(("groups", "tgt", "src", "sub")),
            P(("groups", "tgt", "src", "sub")),
            P("groups", None),
        ),
        check_vma=False,
    )
```

profile of v0, /device:TPU:0, one launch (start us, length us, event | category | flops | bytes accessed | tf_op | source)
XLA Modules:
  0.0 301.9 jit_solution(1247839873346698091)
XLA Ops:
  8.6 1.4 copy.8
  11.1 15.5 %all_gather.6 = bf16[256,300]{1,0:T(8,128)(2,1)S(1)} all-gather(bf16[64,300]{1,0:T(8,128)(2,1)S(1)} %convolution_convert_fusion), channel_id=1, replica_groups=mesh['groups'=2,'tgt'=4,'src'=2,'sub'=2] {'tgt'}, dimensions={0}, use_global_device_ids=true | all-gather | bytes 192000 | tf_op jit(solution)/shard_map/all_gather | solution.py:36
  27.6 5.6 %all_gather.7 = bf16[256,300]{1,0:T(8,128)(2,1)S(1)} all-gather(bf16[64,300]{1,0:T(8,128)(2,1)S(1)} %broadcast_select_fusion), channel_id=1, replica_groups=mesh['groups'=2,'tgt'=4,'src'=2,'sub'=2] {'src','sub'}, dimensions={0}, use_global_device_ids=true | all-gather | bytes 192000 | tf_op jit(solution)/shard_map/all_gather | solution.py:37
  33.6 12.0 %pmax.56 = f32[256]{0:T(256)S(1)} all-reduce(f32[256]{0:T(256)S(1)} %get-tuple-element.8), channel_id=1, replica_groups=mesh['groups'=2,'tgt'=4,'src'=2,'sub'=2] {'tgt'}, use_global_device_ids=true, to_apply=%region_1.3 | all-reduce | flops 256 | bytes 2048 | tf_op jit(solution)/shard_map/pmax | solution.py:16
  45.8 8.4 %psum.63 = f32[256]{0:T(256)S(1)} all-reduce(f32[256]{0:T(256)S(1)} %exponential_reduce_fusion.7), channel_id=1, replica_groups=mesh['groups'=2,'tgt'=4,'src'=2,'sub'=2] {'tgt'}, use_global_device_ids=true, to_apply=%region_3.5 | all-reduce | flops 256 | bytes 2048 | tf_op jit(solution)/shard_map/psum | solution.py:17
  54.3 5.7 %pmax.57 = f32[256]{0:T(256)S(1)} all-reduce(f32[256]{0:T(256)S(1)} %fusion.9), channel_id=1, replica_groups=mesh['groups'=2,'tgt'=4,'src'=2,'sub'=2] {'src','sub'}, use_global_device_ids=true, to_apply=%region_5.7 | all-reduce | flops 256 | bytes 2048 | tf_op jit(solution)/shard_map/pmax | solution.py:22
  60.1 6.6 %psum.64 = f32[256]{0:T(256)S(1)} all-reduce(f32[256]{0:T(256)S(1)} %exponential_reduce_fusion.6), channel_id=1, replica_groups=mesh['groups'=2,'tgt'=4,'src'=2,'sub'=2] {'src','sub'}, use_global_device_ids=true, to_apply=%region_7.9 | all-reduce | flops 256 | bytes 2048 | tf_op jit(solution)/shard_map/psum | solution.py:23
  66.9 10.4 %pmax.58 = f32[256]{0:T(256)S(1)} all-reduce(f32[256]{0:T(256)S(1)} %fusion.10), channel_id=1, replica_groups=mesh['groups'=2,'tgt'=4,'src'=2,'sub'=2] {'tgt'}, use_global_device_ids=true, to_apply=%region_9.11 | all-reduce | flops 256 | bytes 2048 | tf_op jit(solution)/shard_map/pmax | solution.py:16
  77.4 8.4 %psum.65 = f32[256]{0:T(256)S(1)} all-reduce(f32[256]{0:T(256)S(1)} %exponential_reduce_fusion.5), channel_id=1, replica_groups=mesh['groups'=2,'tgt'=4,'src'=2,'sub'=2] {'tgt'}, use_global_device_ids=true, to_apply=%region_11.13 | all-reduce | flops 256 | bytes 2048 | tf_op jit(solution)/shard_map/psum | solution.py:17
  85.9 5.7 %pmax.59 = f32[256]{0:T(256)S(1)} all-reduce(f32[256]{0:T(256)S(1)} %fusion.11), channel_id=1, replica_groups=mesh['groups'=2,'tgt'=4,'src'=2,'sub'=2] {'src','sub'}, use_global_device_ids=true, to_apply=%region_13.15 | all-reduce | flops 256 | bytes 2048 | tf_op jit(solution)/shard_map/pmax | solution.py:22
  91.7 6.3 %psum.66 = f32[256]{0:T(256)S(1)} all-reduce(f32[256]{0:T(256)S(1)} %exponential_reduce_fusion.4), channel_id=1, replica_groups=mesh['groups'=2,'tgt'=4,'src'=2,'sub'=2] {'src','sub'}, use_global_device_ids=true, to_apply=%region_15.17 | all-reduce | flops 256 | bytes 2048 | tf_op jit(solution)/shard_map/psum | solution.py:23
  98.1 10.4 %pmax.60 = f32[256]{0:T(256)S(1)} all-reduce(f32[256]{0:T(256)S(1)} %fusion.12), channel_id=1, replica_groups=mesh['groups'=2,'tgt'=4,'src'=2,'sub'=2] {'tgt'}, use_global_device_ids=true, to_apply=%region_17.19 | all-reduce | flops 256 | bytes 2048 | tf_op jit(solution)/shard_map/pmax | solution.py:16
  108.7 8.4 %psum.67 = f32[256]{0:T(256)S(1)} all-reduce(f32[256]{0:T(256)S(1)} %exponential_reduce_fusion.3), channel_id=1, replica_groups=mesh['groups'=2,'tgt'=4,'src'=2,'sub'=2] {'tgt'}, use_global_device_ids=true, to_apply=%region_19.21 | all-reduce | flops 256 | bytes 2048 | tf_op jit(solution)/shard_map/psum | solution.py:17
  117.2 5.7 %pmax.61 = f32[256]{0:T(256)S(1)} all-reduce(f32[256]{0:T(256)S(1)} %fusion.13), channel_id=1, replica_groups=mesh['groups'=2,'tgt'=4,'src'=2,'sub'=2] {'src','sub'}, use_global_device_ids=true, to_apply=%region_21.23 | all-reduce | flops 256 | bytes 2048 | tf_op jit(solution)/shard_map/pmax | solution.py:22
  123.0 6.5 %psum.68 = f32[256]{0:T(256)S(1)} all-reduce(f32[256]{0:T(256)S(1)} %exponential_reduce_fusion.2), channel_id=1, replica_groups=mesh['groups'=2,'tgt'=4,'src'=2,'sub'=2] {'src','sub'}, use_global_device_ids=true, to_apply=%region_23.25 | all-reduce | flops 256 | bytes 2048 | tf_op jit(solution)/shard_map/psum | solution.py:23
  129.7 10.4 %pmax.62 = f32[256]{0:T(256)S(1)} all-reduce(f32[256]{0:T(256)S(1)} %fusion.14), channel_id=1, replica_groups=mesh['groups'=2,'tgt'=4,'src'=2,'sub'=2] {'tgt'}, use_global_device_ids=true, to_apply=%region_25.27 | all-reduce | flops 256 | bytes 2048 | tf_op jit(solution)/shard_map/pmax | solution.py:16
  140.2 8.4 %psum.69 = f32[256]{0:T(256)S(1)} all-reduce(f32[256]{0:T(256)S(1)} %exponential_reduce_fusion.1), channel_id=1, replica_groups=mesh['groups'=2,'tgt'=4,'src'=2,'sub'=2] {'tgt'}, use_global_device_ids=true, to_apply=%region_27.29 | all-reduce | flops 256 | bytes 2048 | tf_op jit(solution)/shard_map/psum | solution.py:17
  148.7 5.7 %pmax.63 = f32[256]{0:T(256)S(1)} all-reduce(f32[256]{0:T(256)S(1)} %fusion.15), channel_id=1, replica_groups=mesh['groups'=2,'tgt'=4,'src'=2,'sub'=2] {'src','sub'}, use_global_device_ids=true, to_apply=%region_29.31 | all-reduce | flops 256 | bytes 2048 | tf_op jit(solution)/shard_map/pmax | solution.py:22
  154.5 6.3 %psum.70 = f32[256]{0:T(256)S(1)} all-reduce(f32[256]{0:T(256)S(1)} %exponential_reduce_fusion), channel_id=1, replica_groups=mesh['groups'=2,'tgt'=4,'src'=2,'sub'=2] {'src','sub'}, use_global_device_ids=true, to_apply=%region_31.33 | all-reduce | flops 256 | bytes 2048 | tf_op jit(solution)/shard_map/psum | solution.py:23
  162.1 19.8 %reduce-scatter.2.cloned.1.call-done = f32[64,300]{1,0:T(8,128)} async-done(((f32[256,300]{1,0:T(8,128)}), f32[64,300]{1,0:T(8,128)}) %reduce-scatter.2.cloned.1.call-update) | async-done | bytes 76816 | tf_op jit(solution)/shard_map/reduce_scatter | solution.py:56
  181.9 2.1 fusion.22
  185.3 89.6 %all-reduce.2.cloned.1.call-done = f32[300,300]{1,0:T(8,128)} async-done(((f32[300,300]{1,0:T(8,128)}), f32[300,300]{1,0:T(8,128)}) %all-reduce.2.cloned.1.call-update) | async-done | bytes 360016 | tf_op jit(solution)/shard_map/psum | solution.py:65
  274.8 1.8 multiply_reduce_fusion
  293.3 1.8 fusion.1
  (65 shorter events, 24.4 us)
Async XLA Ops:
  7.2 3.6 %copy-start = (f32[300,300]{1,0:T(8,128)S(1)}, f32[300,300]{1,0:T(8,128)}, u32[]{:S(2)}) copy-start(f32[300,300]{1,0:T(8,128)} %param.11) | copy-start | bytes 1080004
  7.2 174.8 %reduce-scatter.2.cloned.1.call-start = ((), (), s32[]{:S(2)}) async-start(), calls=%async_computation.1 | async-start | bytes 491520 | tf_op jit(solution)/shard_map/reduce_scatter | solution.py:56
  7.2 0.7 copy-start.3
  7.9 0.7 copy-start.4
  10.0 16.5 %copy-start.1 = (bf16[784,300]{0,1:T(8,128)(2,1)S(1)}, bf16[784,300]{0,1:T(8,128)(2,1)}, u32[]{:S(2)}) copy-start(bf16[784,300]{0,1:T(8,128)(2,1)} %param.10) | copy-start | bytes 1411204
  161.9 113.0 %all-reduce.2.cloned.1.call-start = ((), (), s32[]{:S(2)}) async-start(), calls=%async_computation.2 | async-start | bytes 933888 | tf_op jit(solution)/shard_map/psum | solution.py:65
  274.8 2.5 copy-start.2
Sparse Core Ops, SparseCore 0:
  162.0 19.8 reduce-scatter.1
  186.3 88.5 all-reduce.1
where the time goes:
time: 303 us; the launch traced here: 302 us
  blocking collectives  146 us (48%)
  waiting for transfers between devices  109 us (36%)
  matrix products  21.5 us (7%)
  between operations  15 us (5%)
  local copies, waits for them, and re-layouts  5.63 us (2%)
  other arithmetic  4.18 us (1%)
    psum x1, waiting for transfers between devices, local(): cov = lax.psum(partial_cov, ('tgt', 'src', 'sub'))  89.6 us
    pmax x4, blocking collectives, row_log_total(): peak = lax.pmax(jnp.max(logits, axis=1), 'tgt')  43.1 us
    psum x4, blocking collectives, row_log_total(): mass = lax.psum(jnp.sum(jnp.exp(logits - peak[:, None]), axis=1), 'tgt')  33.5 us
    psum x4, blocking collectives, col_log_total(): lax.psum(jnp.sum(jnp.exp(logits - peak[None, :]), axis=0), ('src', 'sub'))  25.7 us
    pmax x4, blocking collectives, col_log_total(): peak = lax.pmax(jnp.max(logits, axis=0), ('src', 'sub'))  22.7 us
    reduce_scatter x1, waiting for transfers between devices, local(): lax.psum_scatter(jnp.dot(plan, target_tile, preferred_element_type=jnp.fl...  19.8 us
    all_gather x1, blocking collectives, local(): projected = lax.all_gather(own_projected, 'tgt', axis=0, tiled=True)  15.5 us
    dot_general x8, matrix products, local(): polar = 1.5 * polar - 0.5 * jnp.dot(square, polar, precision=highest)  9.34 us
  transfers between devices with their start and end apart: 2, of which 2 were waited for; matrix products, arithmetic and copies ran while one was open for 0% of the time, Pallas kernels for 0%

commit v1 on v0

--- a/solution.py
+++ b/solution.py
@@ -3,13 +3,19 @@
 import jax
 import jax.numpy as jnp
 from jax import lax
+from jax.experimental import pallas as pl
+from jax.experimental.pallas import tpu as pltpu
 from jax.sharding import PartitionSpec as P
 
 ITERS = 4
 POLAR_STEPS = 8
-
+LANES = 128
+REPLICATED_WORDS = 2048
+VMEM_BYTES = 56 * 1024 * 1024
 
 entropy_scale = 0.05
+
+LOG2_SCALE = math.log2(math.e) / entropy_scale
 
 
 def row_log_total(logits):
@@ -24,7 +30,7 @@
     return peak + jnp.log(mass)
 
 
-def local(src_words, tgt_words, src_vocab, tgt_vocab, mapping):
+def tiled_local(src_words, tgt_words, src_vocab, tgt_vocab, mapping):
     highest = lax.Precision.HIGHEST
     vocab_rows = src_vocab.shape[0]
     place = lax.axis_index(("tgt", "src", "sub"))
@@ -77,6 +83,329 @@
     return (source_potential, target_potential, rotation)
 
 
+def dot32(a, b):
+    return jnp.dot(a, b, preferred_element_type=jnp.float32)
+
+
+def dot_t(a, b):
+    return lax.dot_general(a, b, (((1,), (1,)), ((), ())), preferred_element_type=jnp.float32)
+
+
+def split(a):
+    high = a.astype(jnp.bfloat16)
+    low = (a - high.astype(jnp.float32)).astype(jnp.bfloat16)
+    return high, low
+
+
+def pick_kernel(base_ref, src_ids_ref, tgt_ids_ref, src_ref, tgt_ref, out_ref):
+    rows, count = src_ids_ref.shape[1], src_ref.shape[0]
+    width = src_ref.shape[1]
+    head = width // LANES * LANES
+    tail = width - head
+    base = base_ref[0]
+    diag = lax.broadcasted_iota(jnp.int32, (rows, rows), 0) == lax.broadcasted_iota(
+        jnp.int32, (rows, rows), 1
+    )
+    word = lax.broadcasted_iota(jnp.int32, (rows, count), 1)
+
+    def pick(ids_ref, vocab_ref):
+        ids = jnp.broadcast_to(ids_ref[...] - base, (rows, rows))
+        column = jnp.sum(jnp.where(diag, ids, 0), axis=1, keepdims=True)
+        chosen = jnp.where(word == column, 1.0, 0.0).astype(jnp.bfloat16)
+        return dot32(chosen, vocab_ref[...]).astype(jnp.bfloat16)
+
+    source = pick(src_ids_ref, src_ref)
+    target = pick(tgt_ids_ref, tgt_ref)
+    out_ref[:, :head] = source[:, :head]
+    out_ref[:, head : head + LANES] = jnp.zeros((rows, LANES), jnp.bfloat16)
+    out_ref[:, head : head + tail] = source[:, head:]
+    out_ref[:, head + LANES // 2 : head + LANES // 2 + tail] = target[:, head:]
+    out_ref[:, head + LANES :] = target[:, :head]
+
+
+def transport_kernel(masks, place_ref, mapping_ref, *refs):
+    blocks = refs[: len(masks)]
+    f_ref, g_ref, rot_ref = refs[len(masks) : len(masks) + 3]
+    xy_scr, map_hi, map_lo, xw_scr, k_scr, p_scr, m_scr, u_scr, g_scr, ok_scr = refs[
+        len(masks) + 3 :
+    ]
+    local_rows = blocks[0].shape[0]
+    n = xy_scr.shape[0]
+    width = mapping_ref.shape[0]
+    head = width // LANES * LANES
+    tail = width - head
+    side = head + LANES
+    half = LANES // 2
+    place = place_ref[0]
+    log2n = math.log2(n)
+    mass = 1.0 / n
+    step_rows = 32
+    tiles = n // LANES
+
+    for mask, block in zip(masks, blocks):
+        row = pl.multiple_of((place ^ mask) * local_rows, local_rows)
+        xy_scr[pl.ds(row, local_rows), :] = block[...]
+
+    hi, lo = split(mapping_ref[...])
+    for scr, part in ((map_hi, hi), (map_lo, lo)):
+        scr[...] = jnp.zeros_like(scr)
+        scr[:width, half : half + tail] = part[:, head:]
+        scr[:width, LANES:] = part[:, :head]
+
+    chunk = 256
+    ys = xy_scr[:, head:]
+    for at in range(0, n, chunk):
+        rows = slice(at, at + chunk)
+        xs = xy_scr[rows, :side]
+        xw = (dot32(xs, map_hi[...]) + dot32(xs, map_lo[...])).astype(jnp.bfloat16)
+        xw_scr[rows, :] = xw
+        k_scr[rows, :] = dot_t(xw, ys) * LOG2_SCALE
+
+    def lanes(a):
+        return [a[:, t * LANES : (t + 1) * LANES] for t in range(tiles)]
+
+    def fold(parts, op):
+        parts = list(parts)
+        while len(parts) > 1:
+            parts = [op(a, b) for a, b in zip(parts[::2], parts[1::2])] + (
+                [parts[-1]] if len(parts) % 2 else []
+            )
+        return parts[0]
+
+    def spread(column):
+        return jnp.broadcast_to(column, (column.shape[0], LANES))
+
+    def rows_at(i):
+        return pl.ds(pl.multiple_of(i * step_rows, step_rows), step_rows)
+
+    def fold8(parts):
+        return [fold([a[s : s + 8] for s in range(0, step_rows, 8)], jnp.add) for a in parts]
+
+    def add_all(acc, parts):
+        return tuple(a + b for a, b in zip(acc, fold8(parts)))
+
+    zeros = tuple(jnp.zeros((8, LANES), jnp.float32) for t in range(tiles))
+    inf8 = jnp.full((step_rows, LANES), jnp.inf, jnp.float32)
+
+    def first(i, carry):
+        acc, low, high = carry
+        rows = rows_at(i)
+        parts = lanes(k_scr[rows, :])
+        peak = spread(jnp.max(fold(parts, jnp.maximum), axis=1, keepdims=True))
+        parts = [jnp.exp2(a - peak) for a in parts]
+        r = spread(jnp.sum(fold(parts, jnp.add), axis=1, keepdims=True))
+        u = mass / r
+        for t in range(tiles):
+            k_scr[rows, t * LANES : (t + 1) * LANES] = parts[t]
+        m_scr[rows, :] = peak
+        return add_all(acc, [a * u for a in parts]), jnp.minimum(low, r), jnp.maximum(high, r)
+
+    steps = n // step_rows
+    acc, low, high = lax.fori_loop(0, steps, first, (zeros, inf8, -inf8), unroll=2)
+
+    def close(acc):
+        return [jnp.broadcast_to(jnp.sum(a, axis=0, keepdims=True), (8, LANES)) for a in acc]
+
+    col = close(acc)
+    clow = fold(col, jnp.minimum)
+    chigh = fold(col, jnp.maximum)
+    for it in range(1, ITERS):
+        v = [jnp.concatenate([mass / c] * (step_rows // 8), axis=0) for c in col]
+        last = it == ITERS - 1
+
+        def again(i, carry, v=v, last=last):
+            acc, low, high = carry
+            rows = rows_at(i)
+            parts = lanes(k_scr[rows, :])
+            r = fold([a * b for a, b in zip(parts, v)], jnp.add)
+            r = spread(jnp.sum(r, axis=1, keepdims=True))
+            u = mass / r
+            if last:
+                u_scr[rows, :] = u
+                m_scr[rows, :] = -log2n - m_scr[rows, :] - jnp.log2(r)
+            return add_all(acc, [a * u for a in parts]), jnp.minimum(low, r), jnp.maximum(high, r)
+
+        acc, low, high = lax.fori_loop(0, steps, again, (zeros, low, high), unroll=2)
+        col = close(acc)
+        clow = jnp.minimum(clow, fold(col, jnp.minimum))
+        chigh = jnp.maximum(chigh, fold(col, jnp.maximum))
+
+    for t in range(tiles):
+        g_scr[:, t * LANES : (t + 1) * LANES] = -log2n - jnp.log2(col[t])
+    v = [jnp.concatenate([1.0 / c] * (step_rows // 8), axis=0) for c in col]
+
+    def plan_rows(i, carry):
+        rows = rows_at(i)
+        u = u_scr[rows, :]
+        for t, a in enumerate(lanes(k_scr[rows, :])):
+            p_scr[rows, t * LANES : (t + 1) * LANES] = (a * u * v[t]).astype(jnp.bfloat16)
+        return carry
+
+    lax.fori_loop(0, steps, plan_rows, 0, unroll=2)
+
+    smallest = jnp.minimum(jnp.min(low), jnp.min(clow))
+    largest = jnp.maximum(jnp.max(high), jnp.max(chigh))
+    safe = jnp.logical_and(smallest >= 2.0**-40, largest <= 2.0**40)
+
+    @pl.when(jnp.logical_not(safe))
+    def _():
+        for at in range(0, n, chunk):
+            rows = slice(at, at + chunk)
+            k_scr[rows, :] = dot_t(xw_scr[rows, :], ys) * LOG2_SCALE
+        g_scr[...] = jnp.zeros_like(g_scr)
+
+        def row_step(i, carry):
+            rows = pl.ds(pl.multiple_of(i * 8, 8), 8)
+            logits = k_scr[rows, :] + g_scr[...]
+            peak = jnp.max(logits, axis=1, keepdims=True)
+            r = jnp.sum(jnp.exp2(logits - peak), axis=1, keepdims=True)
+            m_scr[rows, :] = spread(-log2n - peak - jnp.log2(r))
+            return carry
+
+        def logits_of(i):
+            rows = pl.ds(pl.multiple_of(i * 8, 8), 8)
+            return k_scr[rows, :] + jnp.concatenate([m_scr[rows, :]] * tiles, axis=1)
+
+        def iteration(it, carry):
+            lax.fori_loop(0, n // 8, row_step, 0)
+            peak = lax.fori_loop(
+                0,
+                n // 8,
+                lambda i, a: jnp.maximum(a, logits_of(i)),
+                jnp.full((8, n), -jnp.inf, jnp.float32),
+            )
+            peak = jnp.broadcast_to(jnp.max(peak, axis=0, keepdims=True), (8, n))
+            total = lax.fori_loop(
+                0,
+                n // 8,
+                lambda i, a: a + jnp.exp2(logits_of(i) - peak),
+                jnp.zeros((8, n), jnp.float32),
+            )
+            total = jnp.broadcast_to(jnp.sum(total, axis=0, keepdims=True), (8, n))
+            g_scr[...] = -log2n - peak - jnp.log2(total)
+            return carry
+
+        lax.fori_loop(0, ITERS, iteration, 0)
+
+        def plan_step(i, carry):
+            two = [jnp.exp2(logits_of(2 * i + j) + g_scr[...] + log2n) for j in range(2)]
+            rows = pl.ds(pl.multiple_of(i * 16, 16), 16)
+            p_scr[rows, :] = jnp.concatenate(two, axis=0).astype(jnp.bfloat16)
+            return carry
+
+        lax.fori_loop(0, n // 16, plan_step, 0)
+
+    own = pl.ds(pl.multiple_of(place * local_rows, local_rows), local_rows)
+    f = m_scr[own, :]
+    diag = lax.broadcasted_iota(jnp.int32, f.shape, 0) == lax.broadcasted_iota(
+        jnp.int32, f.shape, 1
+    )
+    f = jnp.sum(jnp.where(diag, f, 0.0), axis=0, keepdims=True) * (1.0 / LOG2_SCALE)
+    f_ref[...] = f[:, :local_rows]
+    g = pltpu.roll(g_scr[...], lax.rem(n - place * local_rows, n), 1)
+    g_ref[...] = g[:1, :local_rows] * (1.0 / LOG2_SCALE)
+
+    deep = (width + 15) // 16 * 16
+    cov = jnp.zeros((side, side), jnp.float32)
+    for at in range(0, n, chunk):
+        rows = slice(at, at + chunk)
+        hi, lo = split(dot32(p_scr[rows, :], ys))
+        xs_t = xy_scr[rows, :side].T
+        cov = cov + dot32(xs_t, hi) + dot32(xs_t, lo)
+    cov = cov[:deep]
+    place_y = lax.broadcasted_iota(jnp.int32, (deep, side), 1)
+    cov = jnp.where(place_y >= half, cov, 0.0)
+    q = cov / jnp.sqrt(jnp.sum(cov * cov))
+    for step in range(POLAR_STEPS):
+        hi, lo = split(q)
+        square = dot_t(hi, hi) + dot_t(hi, lo) + dot_t(lo, hi)
+        shi, slo = split(square)
+        q = 1.5 * q - 0.5 * (dot32(shi, hi) + dot32(shi, lo) + dot32(slo, hi))
+    q = q * math.sqrt(width)
+    rot_ref[:, :head] = q[:width, LANES:]
+    rot_ref[:, head:] = q[:width, half : half + tail]
+
+
+def gathered_local(src_words, tgt_words, src_vocab, tgt_vocab, mapping):
+    axes = ("tgt", "src", "sub")
+    sizes = [lax.axis_size(a) for a in axes]
+    local_rows = src_words.shape[0]
+    vocab_rows, width = src_vocab.shape
+    head = width // LANES * LANES
+    side = head + LANES
+    packed = side + head
+    place = lax.axis_index(axes).astype(jnp.int32)
+    vmem = pl.BlockSpec(memory_space=pltpu.VMEM)
+    smem = pl.BlockSpec(memory_space=pltpu.SMEM)
+    own = pl.pallas_call(
+        pick_kernel,
+        out_shape=jax.ShapeDtypeStruct((local_rows, packed), jnp.bfloat16),
+        in_specs=[smem, vmem, vmem, vmem, vmem],
+        out_specs=vmem,
+        compiler_params=pltpu.CompilerParams(vmem_limit_bytes=VMEM_BYTES),
+        name="pick_words",
+    )(
+        (place * vocab_rows).reshape(1),
+        src_words.reshape(1, local_rows),
+        tgt_words.reshape(1, local_rows),
+        src_vocab,
+        tgt_vocab,
+    )
+
+    def swap(a, axis, mask):
+        return lax.ppermute(a, axis, [(i, i ^ mask) for i in range(lax.axis_size(axis))])
+
+    held = {0: own}
+    for axis, below in (("tgt", sizes[1] * sizes[2]), ("src", sizes[2]), ("sub", 1)):
+        for mask in range(1, lax.axis_size(axis)):
+            for key in [k for k in held if (k // below) % lax.axis_size(axis) == 0]:
+                held[key + mask * below] = swap(held[key], axis, mask)
+    masks = sorted(held)
+    n = local_rows * len(masks)
+    f, g, rotation = pl.pallas_call(
+        lambda *refs: transport_kernel(masks, *refs),
+        out_shape=(
+            jax.ShapeDtypeStruct((1, local_rows), jnp.float32),
+            jax.ShapeDtypeStruct((1, local_rows), jnp.float32),
+            jax.ShapeDtypeStruct((width, width), jnp.float32),
+        ),
+        in_specs=[smem, vmem] + [vmem] * len(masks),
+        out_specs=(vmem, vmem, vmem),
+        scratch_shapes=[
+            pltpu.VMEM((n, packed), jnp.bfloat16),
+            pltpu.VMEM((side, side), jnp.bfloat16),
+            pltpu.VMEM((side, side), jnp.bfloat16),
+            pltpu.VMEM((n, side), jnp.bfloat16),
+            pltpu.VMEM((n, n), jnp.float32),
+            pltpu.VMEM((n, n), jnp.bfloat16),
+            pltpu.VMEM((n, LANES), jnp.float32),
+            pltpu.VMEM((n, LANES), jnp.float32),
+            pltpu.VMEM((8, n), jnp.float32),
+            pltpu.SMEM((1,), jnp.int32),
+        ],
+        compiler_params=pltpu.CompilerParams(vmem_limit_bytes=VMEM_BYTES),
+        name="transport",
+    )(place.reshape(1), mapping, *[held[m] for m in masks])
+    return (f.reshape(local_rows), g.reshape(local_rows), rotation)
+
+
+def local(src_words, tgt_words, src_vocab, tgt_vocab, mapping):
+    sizes = [lax.axis_size(a) for a in ("tgt", "src", "sub")]
+    local_rows = src_words.shape[0]
+    total = local_rows * math.prod(sizes)
+    fits = (
+        total <= REPLICATED_WORDS
+        and total % 256 == 0
+        and local_rows % 16 == 0
+        and local_rows <= LANES
+        and all(s & (s - 1) == 0 for s in sizes)
+        and LANES <= src_vocab.shape[1]
+        and 0 < src_vocab.shape[1] % LANES <= LANES // 2
+    )
+    plan = gathered_local if fits else tiled_local
+    return plan(src_words, tgt_words, src_vocab, tgt_vocab, mapping)
+
+
 def solution(mesh):
     placed = (
         P(("groups", "tgt", "src", "sub")),

time: 303 us -> 55.8 us (0.18)
  blocking collectives: 146 us -> 0 us
  waiting for transfers between devices: 109 us -> 7.55 us
  Pallas kernels: 0 us -> 30.9 us
  matrix products: 21.5 us -> 0 us
  between operations: 15 us -> 0.84 us
  starting transfers between devices: 0.26 us -> 12.4 us
  other arithmetic: 4.18 us -> 0 us
    psum x1 -> x0, waiting for transfers between devices: 89.6 us -> none  [local(): cov = lax.psum(partial_cov, ('tgt', 'src', 'sub'))]
    pmax x8 -> x0, blocking collectives: 65.8 us -> none  [the longest x4 43.1 us: row_log_total(): peak = lax.pmax(jnp.max(logits, axis=1), 'tgt')]
    psum x8 -> x0, blocking collectives: 59.1 us -> none  [the longest x4 33.5 us: row_log_total(): mass = lax.psum(jnp.sum(jnp.exp(logits - peak[:, None]), axis=1), 'tgt')]
    pallas_call x0 -> x2, Pallas kernels: none -> 30.9 us  [the longest x1 28.6 us: gathered_local(): pl.pallas_call(lambda *refs: transport_kernel(masks, *refs), out_shape=(j...]
    dot_general x20 -> x0, matrix products: 21.5 us -> none  [the longest x8 9.34 us: local(): polar = 1.5 * polar - 0.5 * jnp.dot(square, polar, precision=highest)]
    all_gather x2 -> x0, blocking collectives: 21.1 us -> none  [the longest x1 15.5 us: local(): projected = lax.all_gather(own_projected, 'tgt', axis=0, tiled=True)]
    reduce_scatter x1 -> x0, waiting for transfers between devices: 19.8 us -> none  [local(): lax.psum_scatter(jnp.dot(plan, target_tile, preferred_element_type=jnp.fl...]
    ppermute x0 -> x15, starting transfers between devices: none -> 12.4 us  [swap(): lax.ppermute(a, axis, [(i, i ^ mask) for i in range(lax.axis_size(axis))])]
  transfers between devices with their start and end apart: 2 -> 15, of which waited for: 2 -> 5; matrix products, arithmetic and copies ran while one was open for 0% -> 0% of each run, Pallas kernels for 0% -> 0%
where the time goes in v1:
time: 55.8 us; the launch traced here: 55.6 us
  Pallas kernels  30.9 us (55%)
  starting transfers between devices  12.4 us (22%)
  waiting for transfers between devices  7.55 us (14%)
  local copies, waits for them, and re-layouts  3.85 us (7%)
  between operations  0.84 us (2%)
    pallas_call x1, Pallas kernels, gathered_local(): pl.pallas_call(lambda *refs: transport_kernel(masks, *refs), out_shape=(j...  28.6 us
    ppermute x15, starting transfers between devices, swap(): lax.ppermute(a, axis, [(i, i ^ mask) for i in range(lax.axis_size(axis))])  12.4 us
    ppermute x15, waiting for transfers between devices, swap(): lax.ppermute(a, axis, [(i, i ^ mask) for i in range(lax.axis_size(axis))])  7.55 us
    unnamed x34, local copies, waits for them, and re-layouts  3.85 us
    pallas_call x1, Pallas kernels, gathered_local(): pl.pallas_call(pick_kernel, out_shape=jax.ShapeDtypeStruct((local_rows, p...  2.38 us
  transfers between devices with their start and end apart: 15, of which 5 were waited for; matrix products, arithmetic and copies ran while one was open for 0% of the time, Pallas kernels for 0%

profile of v1, /device:TPU:0, one launch (start us, length us, event | category | flops | bytes accessed | tf_op | source)
XLA Modules:
  0.0 55.6 jit_solution(1872569930798112026)
XLA Ops:
  0.6 2.2 %copy.8.src_ref = bf16[784,300]{1,0:T(8,128)(2,1)} copy(bf16[784,300]{0,1:T(8,128)(2,1)} %param.7) | data formatting | bytes 940800 | tf_op args[2]
  2.8 1.1 %copy.9.tgt_ref = bf16[784,300]{1,0:T(8,128)(2,1)} copy(bf16[784,300]{0,1:T(8,128)(2,1)S(1)} %copy-done) | data formatting | bytes 940800 | tf_op args[3]
  3.9 2.4 %pick_words.1.refs_2_ = bf16[64,640]{1,0:T(8,128)(2,1)} custom-call(s32[1]{0:T(128)} %bitcast.1.base_ref, s32[1,64]{1,0:T(1,128)} %bitcast.6, s32[1,64]{1,0:T(1,128)} %bitcast.7, bf16[784,300]{1,0:T(8,128)(2,1)} %copy.8.src_ref, bf16[784,300]{1,0:T(8,128)(2,1)} %copy.9.tgt_ref), custom_call_target="tpu_custom_call" | custom-call | tf_op jit(solution)/shard_map/pick_words/pallas_call | solution.py:340
  6.3 5.0 %collective-permute-start.11 = (bf16[64,640]{1,0:T(8,128)(2,1)}, bf16[64,640]{1,0:T(8,128)(2,1)S(1)}, u32[]{:S(2)}, u32[]{:S(2)}) collective-permute-start(bf16[64,640]{1,0:T(8,128)(2,1)} %pick_words.1.refs_2_), channel_id=1, source_target_pairs={{0,12},{4,8},{8,4},{12,0},{1,13},{5,9},{9,5},{13,1},{2,14},{6,10},... | collective-permute-start | bytes 245768 | tf_op jit(solution)/shard_map/ppermute | solution.py:356
  11.4 0.0 collective-permute-start.7
  11.4 0.6 %collective-permute-start.3 = (bf16[64,640]{1,0:T(8,128)(2,1)}, bf16[64,640]{1,0:T(8,128)(2,1)S(1)}, u32[]{:S(2)}, u32[]{:S(2)}) collective-permute-start(bf16[64,640]{1,0:T(8,128)(2,1)} %pick_words.1.refs_2_), channel_id=1, source_target_pairs={{0,4},{4,0},{8,12},{12,8},{1,5},{5,1},{9,13},{13,9},{2,6},{6,2},{1... | collective-permute-start | bytes 245768 | tf_op jit(solution)/shard_map/ppermute | solution.py:356
  11.9 1.7 %collective-permute-start.1 = (bf16[64,640]{1,0:T(8,128)(2,1)}, bf16[64,640]{1,0:T(8,128)(2,1)S(1)}, u32[]{:S(2)}, u32[]{:S(2)}) collective-permute-start(bf16[64,640]{1,0:T(8,128)(2,1)} %pick_words.1.refs_2_), channel_id=1, source_target_pairs={{0,2},{2,0},{1,3},{3,1},{4,6},{6,4},{5,7},{7,5},{8,10},{10,8},{9,1... | collective-permute-start | bytes 245768 | tf_op jit(solution)/shard_map/ppermute | solution.py:356
  13.6 0.9 %collective-permute-done.11.refs_14_ = bf16[64,640]{1,0:T(8,128)(2,1)S(1)} collective-permute-done((bf16[64,640]{1,0:T(8,128)(2,1)}, bf16[64,640]{1,0:T(8,128)(2,1)S(1)}, u32[]{:S(2)}, u32[]{:S(2)}) %collective-permute-start.11) | collective-permute-done | bytes 81952 | tf_op jit(solution)/shard_map/ppermute | solution.py:356
  14.6 1.8 %collective-permute-start.13 = (bf16[64,640]{1,0:T(8,128)(2,1)S(1)}, bf16[64,640]{1,0:T(8,128)(2,1)S(1)}, u32[]{:S(2)}, u32[]{:S(2)}) collective-permute-start(bf16[64,640]{1,0:T(8,128)(2,1)S(1)} %collective-permute-done.11.refs_14_), channel_id=1, source_target_pairs={{0,2},{2,0},{1,3},{3,1},{4,6},{6,4},{5,7},{7,5},{8,10},{10,8},{9,1... | collective-permute-start | bytes 245768 | tf_op jit(solution)/shard_map/ppermute | solution.py:356
  16.3 2.1 %collective-permute-done.7.refs_10_ = bf16[64,640]{1,0:T(8,128)(2,1)S(1)} collective-permute-done((bf16[64,640]{1,0:T(8,128)(2,1)}, bf16[64,640]{1,0:T(8,128)(2,1)S(1)}, u32[]{:S(2)}, u32[]{:S(2)}) %collective-permute-start.7) | collective-permute-done | bytes 81952 | tf_op jit(solution)/shard_map/ppermute | solution.py:356
  18.5 1.6 %collective-permute-start.9 = (bf16[64,640]{1,0:T(8,128)(2,1)S(1)}, bf16[64,640]{1,0:T(8,128)(2,1)S(1)}, u32[]{:S(2)}, u32[]{:S(2)}) collective-permute-start(bf16[64,640]{1,0:T(8,128)(2,1)S(1)} %collective-permute-done.7.refs_10_), channel_id=1, source_target_pairs={{0,2},{2,0},{1,3},{3,1},{4,6},{6,4},{5,7},{7,5},{8,10},{10,8},{9,1... | collective-permute-start | bytes 245768 | tf_op jit(solution)/shard_map/ppermute | solution.py:356
  20.0 0.0 collective-permute-done.1.refs_4_
  20.0 0.2 collective-permute-start.8
  20.2 0.5 collective-permute-start.5
  20.7 0.0 collective-permute-done.13.refs_16_
  20.7 0.1 collective-permute-start.4
  20.8 0.0 collective-permute-done.12.refs_15_
  20.8 0.4 collective-permute-start.2
  21.2 2.2 %collective-permute-done.9.refs_12_ = bf16[64,640]{1,0:T(8,128)(2,1)S(1)} collective-permute-done((bf16[64,640]{1,0:T(8,128)(2,1)S(1)}, bf16[64,640]{1,0:T(8,128)(2,1)S(1)}, u32[]{:S(2)}, u32[]{:S(2)}) %collective-permute-start.9) | collective-permute-done | bytes 81952 | tf_op jit(solution)/shard_map/ppermute | solution.py:356
  23.5 0.5 collective-permute-start.10
  24.0 1.1 %collective-permute-done.5.refs_8_ = bf16[64,640]{1,0:T(8,128)(2,1)S(1)} collective-permute-done((bf16[64,640]{1,0:T(8,128)(2,1)S(1)}, bf16[64,640]{1,0:T(8,128)(2,1)S(1)}, u32[]{:S(2)}, u32[]{:S(2)}) %collective-permute-start.5) | collective-permute-done | bytes 81952 | tf_op jit(solution)/shard_map/ppermute | solution.py:356
  25.2 1.2 %collective-permute-done.6.refs_9_ = bf16[64,640]{1,0:T(8,128)(2,1)S(1)} collective-permute-done((bf16[64,640]{1,0:T(8,128)(2,1)S(1)}, bf16[64,640]{1,0:T(8,128)(2,1)S(1)}, u32[]{:S(2)}, u32[]{:S(2)}) %collective-permute-start.6) | collective-permute-done | bytes 81952 | tf_op jit(solution)/shard_map/ppermute | solution.py:356
  26.5 0.5 copy-done.15
  27.0 28.6 %transport.1 = (f32[1,64]{1,0:T(1,128)}, f32[1,64]{1,0:T(1,128)}, f32[300,300]{1,0:T(8,128)}) custom-call(s32[1]{0:T(128)} %bitcast.refs_0_, f32[300,300]{1,0:T(8,128)} %refs_1_.1, bf16[64,640]{1,0:T(8,128)(2,1)} %pick_words.1.refs_2_, bf16[64,640]{1,0:T(8,128)(2,1)} %copy-done.5, bf16[64,640]{1,0:T(8,128)(2,1)} %copy-done.4, bf16[64,640]{1,0:T(8,128)(2,1)} %copy-done.12, ...), custom_call_target="tpu_custom_call" | custom-call | tf_op jit(solution)/shard_map/transport/pallas_call | solution.py:365
  (42 shorter events, 0.1 us)
Async XLA Ops:
  6.3 8.3 %collective-permute-start.11 = (bf16[64,640]{1,0:T(8,128)(2,1)}, bf16[64,640]{1,0:T(8,128)(2,1)S(1)}, u32[]{:S(2)}, u32[]{:S(2)}) collective-permute-start(bf16[64,640]{1,0:T(8,128)(2,1)} %pick_words.1.refs_2_), channel_id=1, source_target_pairs={{0,12},{4,8},{8,4},{12,0},{1,13},{5,9},{9,5},{13,1},{2,14},{6,10},... | collective-permute-start | bytes 245768 | tf_op jit(solution)/shard_map/ppermute | solution.py:356
  11.4 7.1 %collective-permute-start.7 = (bf16[64,640]{1,0:T(8,128)(2,1)}, bf16[64,640]{1,0:T(8,128)(2,1)S(1)}, u32[]{:S(2)}, u32[]{:S(2)}) collective-permute-start(bf16[64,640]{1,0:T(8,128)(2,1)} %pick_words.1.refs_2_), channel_id=1, source_target_pairs={{0,8},{4,12},{8,0},{12,4},{1,9},{5,13},{9,1},{13,5},{2,10},{6,14},... | collective-permute-start | bytes 245768 | tf_op jit(solution)/shard_map/ppermute | solution.py:356
  11.4 7.1 %collective-permute-start.3 = (bf16[64,640]{1,0:T(8,128)(2,1)}, bf16[64,640]{1,0:T(8,128)(2,1)S(1)}, u32[]{:S(2)}, u32[]{:S(2)}) collective-permute-start(bf16[64,640]{1,0:T(8,128)(2,1)} %pick_words.1.refs_2_), channel_id=1, source_target_pairs={{0,4},{4,0},{8,12},{12,8},{1,5},{5,1},{9,13},{13,9},{2,6},{6,2},{1... | collective-permute-start | bytes 245768 | tf_op jit(solution)/shard_map/ppermute | solution.py:356
  11.9 8.1 %collective-permute-start.1 = (bf16[64,640]{1,0:T(8,128)(2,1)}, bf16[64,640]{1,0:T(8,128)(2,1)S(1)}, u32[]{:S(2)}, u32[]{:S(2)}) collective-permute-start(bf16[64,640]{1,0:T(8,128)(2,1)} %pick_words.1.refs_2_), channel_id=1, source_target_pairs={{0,2},{2,0},{1,3},{3,1},{4,6},{6,4},{5,7},{7,5},{8,10},{10,8},{9,1... | collective-permute-start | bytes 245768 | tf_op jit(solution)/shard_map/ppermute | solution.py:356
  13.6 6.5 %collective-permute-start = (bf16[64,640]{1,0:T(8,128)(2,1)}, bf16[64,640]{1,0:T(8,128)(2,1)S(1)}, u32[]{:S(2)}, u32[]{:S(2)}) collective-permute-start(bf16[64,640]{1,0:T(8,128)(2,1)} %pick_words.1.refs_2_), channel_id=1, source_target_pairs={{0,1},{1,0},{2,3},{3,2},{4,5},{5,4},{6,7},{7,6},{8,9},{9,8},{10,11... | collective-permute-start | bytes 245768 | tf_op jit(solution)/shard_map/ppermute | solution.py:356
  14.6 11.8 %copy-start.1 = (bf16[64,640]{1,0:T(8,128)(2,1)}, bf16[64,640]{1,0:T(8,128)(2,1)S(1)}, u32[]{:S(2)}) copy-start(bf16[64,640]{1,0:T(8,128)(2,1)S(1)} %collective-permute-done.11.refs_14_) | copy-start | bytes 245764
  14.6 6.1 %collective-permute-start.13 = (bf16[64,640]{1,0:T(8,128)(2,1)S(1)}, bf16[64,640]{1,0:T(8,128)(2,1)S(1)}, u32[]{:S(2)}, u32[]{:S(2)}) collective-permute-start(bf16[64,640]{1,0:T(8,128)(2,1)S(1)} %collective-permute-done.11.refs_14_), channel_id=1, source_target_pairs={{0,2},{2,0},{1,3},{3,1},{4,6},{6,4},{5,7},{7,5},{8,10},{10,8},{9,1... | collective-permute-start | bytes 245768 | tf_op jit(solution)/shard_map/ppermute | solution.py:356
  18.4 7.9 %copy-start.2 = (bf16[64,640]{1,0:T(8,128)(2,1)}, bf16[64,640]{1,0:T(8,128)(2,1)S(1)}, u32[]{:S(2)}) copy-start(bf16[64,640]{1,0:T(8,128)(2,1)S(1)} %collective-permute-done.7.refs_10_) | copy-start | bytes 245764
  18.4 2.4 %collective-permute-start.12 = (bf16[64,640]{1,0:T(8,128)(2,1)S(1)}, bf16[64,640]{1,0:T(8,128)(2,1)S(1)}, u32[]{:S(2)}, u32[]{:S(2)}) collective-permute-start(bf16[64,640]{1,0:T(8,128)(2,1)S(1)} %collective-permute-done.11.refs_14_), channel_id=1, source_target_pairs={{0,1},{1,0},{2,3},{3,2},{4,5},{5,4},{6,7},{7,6},{8,9},{9,8},{10,11... | collective-permute-start | bytes 245768 | tf_op jit(solution)/shard_map/ppermute | solution.py:356
  18.4 7.9 %copy-start.3 = (bf16[64,640]{1,0:T(8,128)(2,1)}, bf16[64,640]{1,0:T(8,128)(2,1)S(1)}, u32[]{:S(2)}) copy-start(bf16[64,640]{1,0:T(8,128)(2,1)S(1)} %collective-permute-done.3.refs_6_) | copy-start | bytes 245764
  18.5 5.0 %collective-permute-start.9 = (bf16[64,640]{1,0:T(8,128)(2,1)S(1)}, bf16[64,640]{1,0:T(8,128)(2,1)S(1)}, u32[]{:S(2)}, u32[]{:S(2)}) collective-permute-start(bf16[64,640]{1,0:T(8,128)(2,1)S(1)} %collective-permute-done.7.refs_10_), channel_id=1, source_target_pairs={{0,2},{2,0},{1,3},{3,1},{4,6},{6,4},{5,7},{7,5},{8,10},{10,8},{9,1... | collective-permute-start | bytes 245768 | tf_op jit(solution)/shard_map/ppermute | solution.py:356
  20.0 6.4 %copy-start.4 = (bf16[64,640]{1,0:T(8,128)(2,1)}, bf16[64,640]{1,0:T(8,128)(2,1)S(1)}, u32[]{:S(2)}) copy-start(bf16[64,640]{1,0:T(8,128)(2,1)S(1)} %collective-permute-done.1.refs_4_) | copy-start | bytes 245764
  20.0 3.5 %collective-permute-start.8 = (bf16[64,640]{1,0:T(8,128)(2,1)S(1)}, bf16[64,640]{1,0:T(8,128)(2,1)S(1)}, u32[]{:S(2)}, u32[]{:S(2)}) collective-permute-start(bf16[64,640]{1,0:T(8,128)(2,1)S(1)} %collective-permute-done.7.refs_10_), channel_id=1, source_target_pairs={{0,1},{1,0},{2,3},{3,2},{4,5},{5,4},{6,7},{7,6},{8,9},{9,8},{10,11... | collective-permute-start | bytes 245768 | tf_op jit(solution)/shard_map/ppermute | solution.py:356
  20.2 6.2 %copy-start.5 = (bf16[64,640]{1,0:T(8,128)(2,1)}, bf16[64,640]{1,0:T(8,128)(2,1)S(1)}, u32[]{:S(2)}) copy-start(bf16[64,640]{1,0:T(8,128)(2,1)S(1)} %collective-permute-done.refs_3_) | copy-start | bytes 245764
  20.2 4.9 %collective-permute-start.5 = (bf16[64,640]{1,0:T(8,128)(2,1)S(1)}, bf16[64,640]{1,0:T(8,128)(2,1)S(1)}, u32[]{:S(2)}, u32[]{:S(2)}) collective-permute-start(bf16[64,640]{1,0:T(8,128)(2,1)S(1)} %collective-permute-done.3.refs_6_), channel_id=1, source_target_pairs={{0,2},{2,0},{1,3},{3,1},{4,6},{6,4},{5,7},{7,5},{8,10},{10,8},{9,1... | collective-permute-start | bytes 245768 | tf_op jit(solution)/shard_map/ppermute | solution.py:356
  20.7 5.7 %copy-start.6 = (bf16[64,640]{1,0:T(8,128)(2,1)}, bf16[64,640]{1,0:T(8,128)(2,1)S(1)}, u32[]{:S(2)}) copy-start(bf16[64,640]{1,0:T(8,128)(2,1)S(1)} %collective-permute-done.13.refs_16_) | copy-start | bytes 245764
  20.7 4.3 %collective-permute-start.4 = (bf16[64,640]{1,0:T(8,128)(2,1)S(1)}, bf16[64,640]{1,0:T(8,128)(2,1)S(1)}, u32[]{:S(2)}, u32[]{:S(2)}) collective-permute-start(bf16[64,640]{1,0:T(8,128)(2,1)S(1)} %collective-permute-done.3.refs_6_), channel_id=1, source_target_pairs={{0,1},{1,0},{2,3},{3,2},{4,5},{5,4},{6,7},{7,6},{8,9},{9,8},{10,11... | collective-permute-start | bytes 245768 | tf_op jit(solution)/shard_map/ppermute | solution.py:356
  20.8 5.6 %copy-start.7 = (bf16[64,640]{1,0:T(8,128)(2,1)}, bf16[64,640]{1,0:T(8,128)(2,1)S(1)}, u32[]{:S(2)}) copy-start(bf16[64,640]{1,0:T(8,128)(2,1)S(1)} %collective-permute-done.12.refs_15_) | copy-start | bytes 245764
  20.8 4.3 %collective-permute-start.2 = (bf16[64,640]{1,0:T(8,128)(2,1)S(1)}, bf16[64,640]{1,0:T(8,128)(2,1)S(1)}, u32[]{:S(2)}, u32[]{:S(2)}) collective-permute-start(bf16[64,640]{1,0:T(8,128)(2,1)S(1)} %collective-permute-done.1.refs_4_), channel_id=1, source_target_pairs={{0,1},{1,0},{2,3},{3,2},{4,5},{5,4},{6,7},{7,6},{8,9},{9,8},{10,11... | collective-permute-start | bytes 245768 | tf_op jit(solution)/shard_map/ppermute | solution.py:356
  23.5 2.9 %copy-start.8 = (bf16[64,640]{1,0:T(8,128)(2,1)}, bf16[64,640]{1,0:T(8,128)(2,1)S(1)}, u32[]{:S(2)}) copy-start(bf16[64,640]{1,0:T(8,128)(2,1)S(1)} %collective-permute-done.9.refs_12_) | copy-start | bytes 245764
  23.5 1.6 %collective-permute-start.14 = (bf16[64,640]{1,0:T(8,128)(2,1)S(1)}, bf16[64,640]{1,0:T(8,128)(2,1)S(1)}, u32[]{:S(2)}, u32[]{:S(2)}) collective-permute-start(bf16[64,640]{1,0:T(8,128)(2,1)S(1)} %collective-permute-done.13.refs_16_), channel_id=1, source_target_pairs={{0,1},{1,0},{2,3},{3,2},{4,5},{5,4},{6,7},{7,6},{8,9},{9,8},{10,11... | collective-permute-start | bytes 245768 | tf_op jit(solution)/shard_map/ppermute | solution.py:356
  23.5 2.9 %copy-start.9 = (bf16[64,640]{1,0:T(8,128)(2,1)}, bf16[64,640]{1,0:T(8,128)(2,1)S(1)}, u32[]{:S(2)}) copy-start(bf16[64,640]{1,0:T(8,128)(2,1)S(1)} %collective-permute-done.8.refs_11_) | copy-start | bytes 245764
  23.5 1.6 %collective-permute-start.10 = (bf16[64,640]{1,0:T(8,128)(2,1)S(1)}, bf16[64,640]{1,0:T(8,128)(2,1)S(1)}, u32[]{:S(2)}, u32[]{:S(2)}) collective-permute-start(bf16[64,640]{1,0:T(8,128)(2,1)S(1)} %collective-permute-done.9.refs_12_), channel_id=1, source_target_pairs={{0,1},{1,0},{2,3},{3,2},{4,5},{5,4},{6,7},{7,6},{8,9},{9,8},{10,11... | collective-permute-start | bytes 245768 | tf_op jit(solution)/shard_map/ppermute | solution.py:356
  25.1 1.3 %collective-permute-start.6 = (bf16[64,640]{1,0:T(8,128)(2,1)S(1)}, bf16[64,640]{1,0:T(8,128)(2,1)S(1)}, u32[]{:S(2)}, u32[]{:S(2)}) collective-permute-start(bf16[64,640]{1,0:T(8,128)(2,1)S(1)} %collective-permute-done.5.refs_8_), channel_id=1, source_target_pairs={{0,1},{1,0},{2,3},{3,2},{4,5},{5,4},{6,7},{7,6},{8,9},{9,8},{10,11... | collective-permute-start | bytes 245768 | tf_op jit(solution)/shard_map/ppermute | solution.py:356
  (7 other events, 9.5 us)

commit v2 on v1

--- a/solution.py
+++ b/solution.py
@@ -12,6 +12,7 @@
 LANES = 128
 REPLICATED_WORDS = 2048
 VMEM_BYTES = 56 * 1024 * 1024
+STEP_ROWS = 32
 
 entropy_scale = 0.05
 
@@ -98,8 +99,8 @@
 
 
 def pick_kernel(base_ref, src_ids_ref, tgt_ids_ref, src_ref, tgt_ref, out_ref):
-    rows, count = src_ids_ref.shape[1], src_ref.shape[0]
-    width = src_ref.shape[1]
+    rows = src_ids_ref.shape[1]
+    width, count = src_ref.shape
     head = width // LANES * LANES
     tail = width - head
     base = base_ref[0]
@@ -112,7 +113,7 @@
         ids = jnp.broadcast_to(ids_ref[...] - base, (rows, rows))
         column = jnp.sum(jnp.where(diag, ids, 0), axis=1, keepdims=True)
         chosen = jnp.where(word == column, 1.0, 0.0).astype(jnp.bfloat16)
-        return dot32(chosen, vocab_ref[...]).astype(jnp.bfloat16)
+        return dot_t(chosen, vocab_ref[...]).astype(jnp.bfloat16)
 
     source = pick(src_ids_ref, src_ref)
     target = pick(tgt_ids_ref, tgt_ref)
@@ -139,7 +140,7 @@
     place = place_ref[0]
     log2n = math.log2(n)
     mass = 1.0 / n
-    step_rows = 32
+    step_rows = STEP_ROWS
     tiles = n // LANES
 
     for mask, block in zip(masks, blocks):
@@ -201,7 +202,7 @@
         return add_all(acc, [a * u for a in parts]), jnp.minimum(low, r), jnp.maximum(high, r)
 
     steps = n // step_rows
-    acc, low, high = lax.fori_loop(0, steps, first, (zeros, inf8, -inf8), unroll=2)
+    acc, low, high = lax.fori_loop(0, steps, first, (zeros, inf8, -inf8), unroll=True)
 
     def close(acc):
         return [jnp.broadcast_to(jnp.sum(a, axis=0, keepdims=True), (8, LANES)) for a in acc]
@@ -225,7 +226,7 @@
                 m_scr[rows, :] = -log2n - m_scr[rows, :] - jnp.log2(r)
             return add_all(acc, [a * u for a in parts]), jnp.minimum(low, r), jnp.maximum(high, r)
 
-        acc, low, high = lax.fori_loop(0, steps, again, (zeros, low, high), unroll=2)
+        acc, low, high = lax.fori_loop(0, steps, again, (zeros, low, high), unroll=True)
         col = close(acc)
         clow = jnp.minimum(clow, fold(col, jnp.minimum))
         chigh = jnp.maximum(chigh, fold(col, jnp.maximum))
@@ -241,7 +242,7 @@
             p_scr[rows, t * LANES : (t + 1) * LANES] = (a * u * v[t]).astype(jnp.bfloat16)
         return carry
 
-    lax.fori_loop(0, steps, plan_rows, 0, unroll=2)
+    lax.fori_loop(0, steps, plan_rows, 0, unroll=True)
 
     smallest = jnp.minimum(jnp.min(low), jnp.min(clow))
     largest = jnp.maximum(jnp.max(high), jnp.max(chigh))
@@ -317,10 +318,9 @@
     cov = jnp.where(place_y >= half, cov, 0.0)
     q = cov / jnp.sqrt(jnp.sum(cov * cov))
     for step in range(POLAR_STEPS):
-        hi, lo = split(q)
-        square = dot_t(hi, hi) + dot_t(hi, lo) + dot_t(lo, hi)
-        shi, slo = split(square)
-        q = 1.5 * q - 0.5 * (dot32(shi, hi) + dot32(shi, lo) + dot32(slo, hi))
+        rounded = q.astype(jnp.bfloat16)
+        square = dot_t(rounded, rounded).astype(jnp.bfloat16)
+        q = 1.5 * q - 0.5 * dot32(square, rounded)
     q = q * math.sqrt(width)
     rot_ref[:, :head] = q[:width, LANES:]
     rot_ref[:, head:] = q[:width, half : half + tail]
@@ -348,8 +348,8 @@
         (place * vocab_rows).reshape(1),
         src_words.reshape(1, local_rows),
         tgt_words.reshape(1, local_rows),
-        src_vocab,
-        tgt_vocab,
+        src_vocab.T,
+        tgt_vocab.T,
     )
 
     def swap(a, axis, mask):

time: 55.8 us -> 39.6 us (0.71)
  Pallas kernels: 30.9 us -> 18.1 us
  local copies, waits for them, and re-layouts: 3.85 us -> 0.56 us
    pallas_call x1, Pallas kernels: 28.6 us -> 15.7 us  [gathered_local(): pl.pallas_call(lambda *refs: transport_kernel(masks, *refs), out_shape=(j...]
    unnamed x34 -> x30, local copies, waits for them, and re-layouts: 3.85 us -> 0.56 us
where the time goes in v2:
time: 39.6 us; the launch traced here: 39.4 us
  Pallas kernels  18.1 us (46%)
  starting transfers between devices  12.4 us (31%)
  waiting for transfers between devices  7.55 us (19%)
  between operations  0.83 us (2%)
  local copies, waits for them, and re-layouts  0.56 us (1%)
    pallas_call x1, Pallas kernels, gathered_local(): pl.pallas_call(lambda *refs: transport_kernel(masks, *refs), out_shape=(j...  15.7 us
    ppermute x15, starting transfers between devices, swap(): lax.ppermute(a, axis, [(i, i ^ mask) for i in range(lax.axis_size(axis))])  12.4 us
    ppermute x15, waiting for transfers between devices, swap(): lax.ppermute(a, axis, [(i, i ^ mask) for i in range(lax.axis_size(axis))])  7.55 us
    pallas_call x1, Pallas kernels, gathered_local(): pl.pallas_call(pick_kernel, out_shape=jax.ShapeDtypeStruct((local_rows, p...  2.41 us
  transfers between devices with their start and end apart: 15, of which 5 were waited for; matrix products, arithmetic and copies ran while one was open for 0% of the time, Pallas kernels for 0%

profile of v2, /device:TPU:0, one launch (start us, length us, event | category | flops | bytes accessed | tf_op | source)
XLA Modules:
  0.0 39.4 jit_solution(16059230415148131555)
XLA Ops:
  0.6 2.4 %pick_words.1.refs_2_ = bf16[64,640]{1,0:T(8,128)(2,1)} custom-call(s32[1]{0:T(128)} %bitcast.1.base_ref, s32[1,64]{1,0:T(1,128)} %bitcast.10, s32[1,64]{1,0:T(1,128)} %bitcast.11, bf16[300,784]{1,0:T(8,128)(2,1)} %bitcast.8, bf16[300,784]{1,0:T(8,128)(2,1)} %bitcast.9), custom_call_target="tpu_custom_call" | custom-call | tf_op jit(solution)/shard_map/pick_words/pallas_call | solution.py:340
  3.1 5.0 %collective-permute-start.11 = (bf16[64,640]{1,0:T(8,128)(2,1)}, bf16[64,640]{1,0:T(8,128)(2,1)S(1)}, u32[]{:S(2)}, u32[]{:S(2)}) collective-permute-start(bf16[64,640]{1,0:T(8,128)(2,1)} %pick_words.1.refs_2_), channel_id=1, source_target_pairs={{0,12},{4,8},{8,4},{12,0},{1,13},{5,9},{9,5},{13,1},{2,14},{6,10},... | collective-permute-start | bytes 245768 | tf_op jit(solution)/shard_map/ppermute | solution.py:356
  8.1 0.0 collective-permute-start.7
  8.1 0.6 %collective-permute-start.3 = (bf16[64,640]{1,0:T(8,128)(2,1)}, bf16[64,640]{1,0:T(8,128)(2,1)S(1)}, u32[]{:S(2)}, u32[]{:S(2)}) collective-permute-start(bf16[64,640]{1,0:T(8,128)(2,1)} %pick_words.1.refs_2_), channel_id=1, source_target_pairs={{0,4},{4,0},{8,12},{12,8},{1,5},{5,1},{9,13},{13,9},{2,6},{6,2},{1... | collective-permute-start | bytes 245768 | tf_op jit(solution)/shard_map/ppermute | solution.py:356
  8.7 1.7 %collective-permute-start.1 = (bf16[64,640]{1,0:T(8,128)(2,1)}, bf16[64,640]{1,0:T(8,128)(2,1)S(1)}, u32[]{:S(2)}, u32[]{:S(2)}) collective-permute-start(bf16[64,640]{1,0:T(8,128)(2,1)} %pick_words.1.refs_2_), channel_id=1, source_target_pairs={{0,2},{2,0},{1,3},{3,1},{4,6},{6,4},{5,7},{7,5},{8,10},{10,8},{9,1... | collective-permute-start | bytes 245768 | tf_op jit(solution)/shard_map/ppermute | solution.py:356
  10.4 0.9 %collective-permute-done.11.refs_14_ = bf16[64,640]{1,0:T(8,128)(2,1)S(1)} collective-permute-done((bf16[64,640]{1,0:T(8,128)(2,1)}, bf16[64,640]{1,0:T(8,128)(2,1)S(1)}, u32[]{:S(2)}, u32[]{:S(2)}) %collective-permute-start.11) | collective-permute-done | bytes 81952 | tf_op jit(solution)/shard_map/ppermute | solution.py:356
  11.3 1.8 %collective-permute-start.13 = (bf16[64,640]{1,0:T(8,128)(2,1)S(1)}, bf16[64,640]{1,0:T(8,128)(2,1)S(1)}, u32[]{:S(2)}, u32[]{:S(2)}) collective-permute-start(bf16[64,640]{1,0:T(8,128)(2,1)S(1)} %collective-permute-done.11.refs_14_), channel_id=1, source_target_pairs={{0,2},{2,0},{1,3},{3,1},{4,6},{6,4},{5,7},{7,5},{8,10},{10,8},{9,1... | collective-permute-start | bytes 245768 | tf_op jit(solution)/shard_map/ppermute | solution.py:356
  13.1 2.1 %collective-permute-done.7.refs_10_ = bf16[64,640]{1,0:T(8,128)(2,1)S(1)} collective-permute-done((bf16[64,640]{1,0:T(8,128)(2,1)}, bf16[64,640]{1,0:T(8,128)(2,1)S(1)}, u32[]{:S(2)}, u32[]{:S(2)}) %collective-permute-start.7) | collective-permute-done | bytes 81952 | tf_op jit(solution)/shard_map/ppermute | solution.py:356
  15.2 0.0 collective-permute-start.12
  15.2 1.6 %collective-permute-start.9 = (bf16[64,640]{1,0:T(8,128)(2,1)S(1)}, bf16[64,640]{1,0:T(8,128)(2,1)S(1)}, u32[]{:S(2)}, u32[]{:S(2)}) collective-permute-start(bf16[64,640]{1,0:T(8,128)(2,1)S(1)} %collective-permute-done.7.refs_10_), channel_id=1, source_target_pairs={{0,2},{2,0},{1,3},{3,1},{4,6},{6,4},{5,7},{7,5},{8,10},{10,8},{9,1... | collective-permute-start | bytes 245768 | tf_op jit(solution)/shard_map/ppermute | solution.py:356
  16.8 0.0 collective-permute-done.1.refs_4_
  16.8 0.2 collective-permute-start.8
  16.9 0.0 collective-permute-done.refs_3_
  16.9 0.5 %collective-permute-start.5 = (bf16[64,640]{1,0:T(8,128)(2,1)S(1)}, bf16[64,640]{1,0:T(8,128)(2,1)S(1)}, u32[]{:S(2)}, u32[]{:S(2)}) collective-permute-start(bf16[64,640]{1,0:T(8,128)(2,1)S(1)} %collective-permute-done.3.refs_6_), channel_id=1, source_target_pairs={{0,2},{2,0},{1,3},{3,1},{4,6},{6,4},{5,7},{7,5},{8,10},{10,8},{9,1... | collective-permute-start | bytes 245768 | tf_op jit(solution)/shard_map/ppermute | solution.py:356
  17.5 0.1 collective-permute-start.4
  17.5 0.4 %collective-permute-start.2 = (bf16[64,640]{1,0:T(8,128)(2,1)S(1)}, bf16[64,640]{1,0:T(8,128)(2,1)S(1)}, u32[]{:S(2)}, u32[]{:S(2)}) collective-permute-start(bf16[64,640]{1,0:T(8,128)(2,1)S(1)} %collective-permute-done.1.refs_4_), channel_id=1, source_target_pairs={{0,1},{1,0},{2,3},{3,2},{4,5},{5,4},{6,7},{7,6},{8,9},{9,8},{10,11... | collective-permute-start | bytes 245768 | tf_op jit(solution)/shard_map/ppermute | solution.py:356
  18.0 2.2 %collective-permute-done.9.refs_12_ = bf16[64,640]{1,0:T(8,128)(2,1)S(1)} collective-permute-done((bf16[64,640]{1,0:T(8,128)(2,1)S(1)}, bf16[64,640]{1,0:T(8,128)(2,1)S(1)}, u32[]{:S(2)}, u32[]{:S(2)}) %collective-permute-start.9) | collective-permute-done | bytes 81952 | tf_op jit(solution)/shard_map/ppermute | solution.py:356
  20.3 0.5 %collective-permute-start.10 = (bf16[64,640]{1,0:T(8,128)(2,1)S(1)}, bf16[64,640]{1,0:T(8,128)(2,1)S(1)}, u32[]{:S(2)}, u32[]{:S(2)}) collective-permute-start(bf16[64,640]{1,0:T(8,128)(2,1)S(1)} %collective-permute-done.9.refs_12_), channel_id=1, source_target_pairs={{0,1},{1,0},{2,3},{3,2},{4,5},{5,4},{6,7},{7,6},{8,9},{9,8},{10,11... | collective-permute-start | bytes 245768 | tf_op jit(solution)/shard_map/ppermute | solution.py:356
  20.8 1.1 %collective-permute-done.5.refs_8_ = bf16[64,640]{1,0:T(8,128)(2,1)S(1)} collective-permute-done((bf16[64,640]{1,0:T(8,128)(2,1)S(1)}, bf16[64,640]{1,0:T(8,128)(2,1)S(1)}, u32[]{:S(2)}, u32[]{:S(2)}) %collective-permute-start.5) | collective-permute-done | bytes 81952 | tf_op jit(solution)/shard_map/ppermute | solution.py:356
  21.8 0.0 collective-permute-done.2.refs_5_
  21.9 0.0 collective-permute-done.14.refs_17_
  21.9 1.2 %collective-permute-done.6.refs_9_ = bf16[64,640]{1,0:T(8,128)(2,1)S(1)} collective-permute-done((bf16[64,640]{1,0:T(8,128)(2,1)S(1)}, bf16[64,640]{1,0:T(8,128)(2,1)S(1)}, u32[]{:S(2)}, u32[]{:S(2)}) %collective-permute-start.6) | collective-permute-done | bytes 81952 | tf_op jit(solution)/shard_map/ppermute | solution.py:356
  23.2 0.5 %copy-done.14 = bf16[64,640]{1,0:T(8,128)(2,1)} copy-done((bf16[64,640]{1,0:T(8,128)(2,1)}, bf16[64,640]{1,0:T(8,128)(2,1)S(1)}, u32[]{:S(2)}) %copy-start.14) | copy-done | bytes 81944
  23.7 15.7 %transport.1 = (f32[1,64]{1,0:T(1,128)}, f32[1,64]{1,0:T(1,128)}, f32[300,300]{1,0:T(8,128)}) custom-call(s32[1]{0:T(128)} %bitcast.refs_0_, f32[300,300]{1,0:T(8,128)} %refs_1_.1, bf16[64,640]{1,0:T(8,128)(2,1)} %pick_words.1.refs_2_, bf16[64,640]{1,0:T(8,128)(2,1)} %copy-done.4, bf16[64,640]{1,0:T(8,128)(2,1)} %copy-done.3, bf16[64,640]{1,0:T(8,128)(2,1)} %copy-done.11, ...), custom_call_target="tpu_custom_call" | custom-call | tf_op jit(solution)/shard_map/transport/pallas_call | solution.py:365
  (38 shorter events, 0.1 us)
Async XLA Ops:
  3.1 8.3 %collective-permute-start.11 = (bf16[64,640]{1,0:T(8,128)(2,1)}, bf16[64,640]{1,0:T(8,128)(2,1)S(1)}, u32[]{:S(2)}, u32[]{:S(2)}) collective-permute-start(bf16[64,640]{1,0:T(8,128)(2,1)} %pick_words.1.refs_2_), channel_id=1, source_target_pairs={{0,12},{4,8},{8,4},{12,0},{1,13},{5,9},{9,5},{13,1},{2,14},{6,10},... | collective-permute-start | bytes 245768 | tf_op jit(solution)/shard_map/ppermute | solution.py:356
  8.1 7.1 %collective-permute-start.7 = (bf16[64,640]{1,0:T(8,128)(2,1)}, bf16[64,640]{1,0:T(8,128)(2,1)S(1)}, u32[]{:S(2)}, u32[]{:S(2)}) collective-permute-start(bf16[64,640]{1,0:T(8,128)(2,1)} %pick_words.1.refs_2_), channel_id=1, source_target_pairs={{0,8},{4,12},{8,0},{12,4},{1,9},{5,13},{9,1},{13,5},{2,10},{6,14},... | collective-permute-start | bytes 245768 | tf_op jit(solution)/shard_map/ppermute | solution.py:356
  8.1 7.1 %collective-permute-start.3 = (bf16[64,640]{1,0:T(8,128)(2,1)}, bf16[64,640]{1,0:T(8,128)(2,1)S(1)}, u32[]{:S(2)}, u32[]{:S(2)}) collective-permute-start(bf16[64,640]{1,0:T(8,128)(2,1)} %pick_words.1.refs_2_), channel_id=1, source_target_pairs={{0,4},{4,0},{8,12},{12,8},{1,5},{5,1},{9,13},{13,9},{2,6},{6,2},{1... | collective-permute-start | bytes 245768 | tf_op jit(solution)/shard_map/ppermute | solution.py:356
  8.7 8.1 %collective-permute-start.1 = (bf16[64,640]{1,0:T(8,128)(2,1)}, bf16[64,640]{1,0:T(8,128)(2,1)S(1)}, u32[]{:S(2)}, u32[]{:S(2)}) collective-permute-start(bf16[64,640]{1,0:T(8,128)(2,1)} %pick_words.1.refs_2_), channel_id=1, source_target_pairs={{0,2},{2,0},{1,3},{3,1},{4,6},{6,4},{5,7},{7,5},{8,10},{10,8},{9,1... | collective-permute-start | bytes 245768 | tf_op jit(solution)/shard_map/ppermute | solution.py:356
  10.4 6.5 %collective-permute-start = (bf16[64,640]{1,0:T(8,128)(2,1)}, bf16[64,640]{1,0:T(8,128)(2,1)S(1)}, u32[]{:S(2)}, u32[]{:S(2)}) collective-permute-start(bf16[64,640]{1,0:T(8,128)(2,1)} %pick_words.1.refs_2_), channel_id=1, source_target_pairs={{0,1},{1,0},{2,3},{3,2},{4,5},{5,4},{6,7},{7,6},{8,9},{9,8},{10,11... | collective-permute-start | bytes 245768 | tf_op jit(solution)/shard_map/ppermute | solution.py:356
  11.3 11.8 %copy-start = (bf16[64,640]{1,0:T(8,128)(2,1)}, bf16[64,640]{1,0:T(8,128)(2,1)S(1)}, u32[]{:S(2)}) copy-start(bf16[64,640]{1,0:T(8,128)(2,1)S(1)} %collective-permute-done.11.refs_14_) | copy-start | bytes 245764
  11.3 6.1 %collective-permute-start.13 = (bf16[64,640]{1,0:T(8,128)(2,1)S(1)}, bf16[64,640]{1,0:T(8,128)(2,1)S(1)}, u32[]{:S(2)}, u32[]{:S(2)}) collective-permute-start(bf16[64,640]{1,0:T(8,128)(2,1)S(1)} %collective-permute-done.11.refs_14_), channel_id=1, source_target_pairs={{0,2},{2,0},{1,3},{3,1},{4,6},{6,4},{5,7},{7,5},{8,10},{10,8},{9,1... | collective-permute-start | bytes 245768 | tf_op jit(solution)/shard_map/ppermute | solution.py:356
  15.2 7.9 %copy-start.1 = (bf16[64,640]{1,0:T(8,128)(2,1)}, bf16[64,640]{1,0:T(8,128)(2,1)S(1)}, u32[]{:S(2)}) copy-start(bf16[64,640]{1,0:T(8,128)(2,1)S(1)} %collective-permute-done.7.refs_10_) | copy-start | bytes 245764
  15.2 2.4 %collective-permute-start.12 = (bf16[64,640]{1,0:T(8,128)(2,1)S(1)}, bf16[64,640]{1,0:T(8,128)(2,1)S(1)}, u32[]{:S(2)}, u32[]{:S(2)}) collective-permute-start(bf16[64,640]{1,0:T(8,128)(2,1)S(1)} %collective-permute-done.11.refs_14_), channel_id=1, source_target_pairs={{0,1},{1,0},{2,3},{3,2},{4,5},{5,4},{6,7},{7,6},{8,9},{9,8},{10,11... | collective-permute-start | bytes 245768 | tf_op jit(solution)/shard_map/ppermute | solution.py:356
  15.2 7.9 %copy-start.2 = (bf16[64,640]{1,0:T(8,128)(2,1)}, bf16[64,640]{1,0:T(8,128)(2,1)S(1)}, u32[]{:S(2)}) copy-start(bf16[64,640]{1,0:T(8,128)(2,1)S(1)} %collective-permute-done.3.refs_6_) | copy-start | bytes 245764
  15.2 5.0 %collective-permute-start.9 = (bf16[64,640]{1,0:T(8,128)(2,1)S(1)}, bf16[64,640]{1,0:T(8,128)(2,1)S(1)}, u32[]{:S(2)}, u32[]{:S(2)}) collective-permute-start(bf16[64,640]{1,0:T(8,128)(2,1)S(1)} %collective-permute-done.7.refs_10_), channel_id=1, source_target_pairs={{0,2},{2,0},{1,3},{3,1},{4,6},{6,4},{5,7},{7,5},{8,10},{10,8},{9,1... | collective-permute-start | bytes 245768 | tf_op jit(solution)/shard_map/ppermute | solution.py:356
  16.8 6.4 %copy-start.3 = (bf16[64,640]{1,0:T(8,128)(2,1)}, bf16[64,640]{1,0:T(8,128)(2,1)S(1)}, u32[]{:S(2)}) copy-start(bf16[64,640]{1,0:T(8,128)(2,1)S(1)} %collective-permute-done.1.refs_4_) | copy-start | bytes 245764
  16.8 3.5 %collective-permute-start.8 = (bf16[64,640]{1,0:T(8,128)(2,1)S(1)}, bf16[64,640]{1,0:T(8,128)(2,1)S(1)}, u32[]{:S(2)}, u32[]{:S(2)}) collective-permute-start(bf16[64,640]{1,0:T(8,128)(2,1)S(1)} %collective-permute-done.7.refs_10_), channel_id=1, source_target_pairs={{0,1},{1,0},{2,3},{3,2},{4,5},{5,4},{6,7},{7,6},{8,9},{9,8},{10,11... | collective-permute-start | bytes 245768 | tf_op jit(solution)/shard_map/ppermute | solution.py:356
  16.9 6.2 %copy-start.4 = (bf16[64,640]{1,0:T(8,128)(2,1)}, bf16[64,640]{1,0:T(8,128)(2,1)S(1)}, u32[]{:S(2)}) copy-start(bf16[64,640]{1,0:T(8,128)(2,1)S(1)} %collective-permute-done.refs_3_) | copy-start | bytes 245764
  16.9 4.9 %collective-permute-start.5 = (bf16[64,640]{1,0:T(8,128)(2,1)S(1)}, bf16[64,640]{1,0:T(8,128)(2,1)S(1)}, u32[]{:S(2)}, u32[]{:S(2)}) collective-permute-start(bf16[64,640]{1,0:T(8,128)(2,1)S(1)} %collective-permute-done.3.refs_6_), channel_id=1, source_target_pairs={{0,2},{2,0},{1,3},{3,1},{4,6},{6,4},{5,7},{7,5},{8,10},{10,8},{9,1... | collective-permute-start | bytes 245768 | tf_op jit(solution)/shard_map/ppermute | solution.py:356
  17.5 5.7 %copy-start.5 = (bf16[64,640]{1,0:T(8,128)(2,1)}, bf16[64,640]{1,0:T(8,128)(2,1)S(1)}, u32[]{:S(2)}) copy-start(bf16[64,640]{1,0:T(8,128)(2,1)S(1)} %collective-permute-done.13.refs_16_) | copy-start | bytes 245764
  17.5 4.3 %collective-permute-start.4 = (bf16[64,640]{1,0:T(8,128)(2,1)S(1)}, bf16[64,640]{1,0:T(8,128)(2,1)S(1)}, u32[]{:S(2)}, u32[]{:S(2)}) collective-permute-start(bf16[64,640]{1,0:T(8,128)(2,1)S(1)} %collective-permute-done.3.refs_6_), channel_id=1, source_target_pairs={{0,1},{1,0},{2,3},{3,2},{4,5},{5,4},{6,7},{7,6},{8,9},{9,8},{10,11... | collective-permute-start | bytes 245768 | tf_op jit(solution)/shard_map/ppermute | solution.py:356
  17.5 5.6 %copy-start.6 = (bf16[64,640]{1,0:T(8,128)(2,1)}, bf16[64,640]{1,0:T(8,128)(2,1)S(1)}, u32[]{:S(2)}) copy-start(bf16[64,640]{1,0:T(8,128)(2,1)S(1)} %collective-permute-done.12.refs_15_) | copy-start | bytes 245764
  17.5 4.3 %collective-permute-start.2 = (bf16[64,640]{1,0:T(8,128)(2,1)S(1)}, bf16[64,640]{1,0:T(8,128)(2,1)S(1)}, u32[]{:S(2)}, u32[]{:S(2)}) collective-permute-start(bf16[64,640]{1,0:T(8,128)(2,1)S(1)} %collective-permute-done.1.refs_4_), channel_id=1, source_target_pairs={{0,1},{1,0},{2,3},{3,2},{4,5},{5,4},{6,7},{7,6},{8,9},{9,8},{10,11... | collective-permute-start | bytes 245768 | tf_op jit(solution)/shard_map/ppermute | solution.py:356
  20.2 2.9 %copy-start.7 = (bf16[64,640]{1,0:T(8,128)(2,1)}, bf16[64,640]{1,0:T(8,128)(2,1)S(1)}, u32[]{:S(2)}) copy-start(bf16[64,640]{1,0:T(8,128)(2,1)S(1)} %collective-permute-done.9.refs_12_) | copy-start | bytes 245764
  20.2 1.6 %collective-permute-start.14 = (bf16[64,640]{1,0:T(8,128)(2,1)S(1)}, bf16[64,640]{1,0:T(8,128)(2,1)S(1)}, u32[]{:S(2)}, u32[]{:S(2)}) collective-permute-start(bf16[64,640]{1,0:T(8,128)(2,1)S(1)} %collective-permute-done.13.refs_16_), channel_id=1, source_target_pairs={{0,1},{1,0},{2,3},{3,2},{4,5},{5,4},{6,7},{7,6},{8,9},{9,8},{10,11... | collective-permute-start | bytes 245768 | tf_op jit(solution)/shard_map/ppermute | solution.py:356
  20.2 2.9 %copy-start.8 = (bf16[64,640]{1,0:T(8,128)(2,1)}, bf16[64,640]{1,0:T(8,128)(2,1)S(1)}, u32[]{:S(2)}) copy-start(bf16[64,640]{1,0:T(8,128)(2,1)S(1)} %collective-permute-done.8.refs_11_) | copy-start | bytes 245764
  20.3 1.6 %collective-permute-start.10 = (bf16[64,640]{1,0:T(8,128)(2,1)S(1)}, bf16[64,640]{1,0:T(8,128)(2,1)S(1)}, u32[]{:S(2)}, u32[]{:S(2)}) collective-permute-start(bf16[64,640]{1,0:T(8,128)(2,1)S(1)} %collective-permute-done.9.refs_12_), channel_id=1, source_target_pairs={{0,1},{1,0},{2,3},{3,2},{4,5},{5,4},{6,7},{7,6},{8,9},{9,8},{10,11... | collective-permute-start | bytes 245768 | tf_op jit(solution)/shard_map/ppermute | solution.py:356
  21.8 1.3 %collective-permute-start.6 = (bf16[64,640]{1,0:T(8,128)(2,1)S(1)}, bf16[64,640]{1,0:T(8,128)(2,1)S(1)}, u32[]{:S(2)}, u32[]{:S(2)}) collective-permute-start(bf16[64,640]{1,0:T(8,128)(2,1)S(1)} %collective-permute-done.5.refs_8_), channel_id=1, source_target_pairs={{0,1},{1,0},{2,3},{3,2},{4,5},{5,4},{6,7},{7,6},{8,9},{9,8},{10,11... | collective-permute-start | bytes 245768 | tf_op jit(solution)/shard_map/ppermute | solution.py:356
  (6 other events, 7.3 us)

commit v3 on v2

--- a/solution.py
+++ b/solution.py
@@ -12,6 +12,7 @@
 LANES = 128
 REPLICATED_WORDS = 2048
 VMEM_BYTES = 56 * 1024 * 1024
+KERNEL_VMEM_BYTES = 20 * 1024 * 1024
 STEP_ROWS = 32
 
 entropy_scale = 0.05
@@ -104,16 +105,12 @@
     head = width // LANES * LANES
     tail = width - head
     base = base_ref[0]
-    diag = lax.broadcasted_iota(jnp.int32, (rows, rows), 0) == lax.broadcasted_iota(
-        jnp.int32, (rows, rows), 1
-    )
-    word = lax.broadcasted_iota(jnp.int32, (rows, count), 1)
+    word = lax.broadcasted_iota(jnp.int32, (count, rows), 0)
 
     def pick(ids_ref, vocab_ref):
-        ids = jnp.broadcast_to(ids_ref[...] - base, (rows, rows))
-        column = jnp.sum(jnp.where(diag, ids, 0), axis=1, keepdims=True)
-        chosen = jnp.where(word == column, 1.0, 0.0).astype(jnp.bfloat16)
-        return dot_t(chosen, vocab_ref[...]).astype(jnp.bfloat16)
+        ids = jnp.broadcast_to(ids_ref[...] - base, (count, rows))
+        chosen = jnp.where(word == ids, 1.0, 0.0).astype(jnp.bfloat16)
+        return dot32(vocab_ref[...], chosen).T.astype(jnp.bfloat16)
 
     source = pick(src_ids_ref, src_ref)
     target = pick(tgt_ids_ref, tgt_ref)
@@ -127,7 +124,7 @@
 def transport_kernel(masks, place_ref, mapping_ref, *refs):
     blocks = refs[: len(masks)]
     f_ref, g_ref, rot_ref = refs[len(masks) : len(masks) + 3]
-    xy_scr, map_hi, map_lo, xw_scr, k_scr, p_scr, m_scr, u_scr, g_scr, ok_scr = refs[
+    xy_scr, map_hi, map_lo, xw_scr, k_scr, p_scr, m_scr, u_scr, g_scr, cov_scr, sems = refs[
         len(masks) + 3 :
     ]
     local_rows = blocks[0].shape[0]
@@ -143,9 +140,13 @@
     step_rows = STEP_ROWS
     tiles = n // LANES
 
-    for mask, block in zip(masks, blocks):
+    copies = []
+    for at, (mask, block) in enumerate(zip(masks, blocks)):
         row = pl.multiple_of((place ^ mask) * local_rows, local_rows)
-        xy_scr[pl.ds(row, local_rows), :] = block[...]
+        copies.append(
+            pltpu.make_async_copy(block, xy_scr.at[pl.ds(row, local_rows), :], sems.at[at])
+        )
+        copies[-1].start()
 
     hi, lo = split(mapping_ref[...])
     for scr, part in ((map_hi, hi), (map_lo, lo)):
@@ -153,14 +154,11 @@
         scr[:width, half : half + tail] = part[:, head:]
         scr[:width, LANES:] = part[:, :head]
 
+    for copy in copies:
+        copy.wait()
+
     chunk = 256
     ys = xy_scr[:, head:]
-    for at in range(0, n, chunk):
-        rows = slice(at, at + chunk)
-        xs = xy_scr[rows, :side]
-        xw = (dot32(xs, map_hi[...]) + dot32(xs, map_lo[...])).astype(jnp.bfloat16)
-        xw_scr[rows, :] = xw
-        k_scr[rows, :] = dot_t(xw, ys) * LOG2_SCALE
 
     def lanes(a):
         return [a[:, t * LANES : (t + 1) * LANES] for t in range(tiles)]
@@ -177,7 +175,7 @@
         return jnp.broadcast_to(column, (column.shape[0], LANES))
 
     def rows_at(i):
-        return pl.ds(pl.multiple_of(i * step_rows, step_rows), step_rows)
+        return pl.ds(i * step_rows, step_rows)
 
     def fold8(parts):
         return [fold([a[s : s + 8] for s in range(0, step_rows, 8)], jnp.add) for a in parts]
@@ -193,16 +191,27 @@
         rows = rows_at(i)
         parts = lanes(k_scr[rows, :])
         peak = spread(jnp.max(fold(parts, jnp.maximum), axis=1, keepdims=True))
-        parts = [jnp.exp2(a - peak) for a in parts]
+        parts = [jnp.exp2((a - peak) * LOG2_SCALE) for a in parts]
         r = spread(jnp.sum(fold(parts, jnp.add), axis=1, keepdims=True))
         u = mass / r
         for t in range(tiles):
             k_scr[rows, t * LANES : (t + 1) * LANES] = parts[t]
-        m_scr[rows, :] = peak
+        m_scr[rows, :] = peak * LOG2_SCALE
         return add_all(acc, [a * u for a in parts]), jnp.minimum(low, r), jnp.maximum(high, r)
 
     steps = n // step_rows
-    acc, low, high = lax.fori_loop(0, steps, first, (zeros, inf8, -inf8), unroll=True)
+    carry = (zeros, inf8, -inf8)
+    map_all = jnp.concatenate([map_hi[:head], map_lo[:head], map_hi[head:], map_lo[head:]], axis=0)
+    for at in range(0, n, chunk):
+        rows = slice(at, at + chunk)
+        xs = xy_scr[rows, :side]
+        sides = [xs[:, :head], xs[:, :head], xs[:, head:], xs[:, head:]]
+        xw = dot32(jnp.concatenate(sides, axis=1), map_all).astype(jnp.bfloat16)
+        xw_scr[rows, :] = xw
+        k_scr[rows, :] = dot_t(xw, ys)
+        for i in range(at // step_rows, (at + chunk) // step_rows):
+            carry = first(i, carry)
+    acc, low, high = carry
 
     def close(acc):
         return [jnp.broadcast_to(jnp.sum(a, axis=0, keepdims=True), (8, LANES)) for a in acc]
@@ -226,7 +235,10 @@
                 m_scr[rows, :] = -log2n - m_scr[rows, :] - jnp.log2(r)
             return add_all(acc, [a * u for a in parts]), jnp.minimum(low, r), jnp.maximum(high, r)
 
-        acc, low, high = lax.fori_loop(0, steps, again, (zeros, low, high), unroll=True)
+        carry = (zeros, low, high)
+        for i in range(steps):
+            carry = again(i, carry)
+        acc, low, high = carry
         col = close(acc)
         clow = jnp.minimum(clow, fold(col, jnp.minimum))
         chigh = jnp.maximum(chigh, fold(col, jnp.maximum))
@@ -235,14 +247,18 @@
         g_scr[:, t * LANES : (t + 1) * LANES] = -log2n - jnp.log2(col[t])
     v = [jnp.concatenate([1.0 / c] * (step_rows // 8), axis=0) for c in col]
 
-    def plan_rows(i, carry):
+    deep = (width + 15) // 16 * 16
+
+    def covariance():
+        bary = dot32(p_scr[...], ys).astype(jnp.bfloat16)
+        return dot32(xy_scr[:, :side].T, bary)[:deep]
+
+    for i in range(steps):
         rows = rows_at(i)
         u = u_scr[rows, :]
         for t, a in enumerate(lanes(k_scr[rows, :])):
             p_scr[rows, t * LANES : (t + 1) * LANES] = (a * u * v[t]).astype(jnp.bfloat16)
-        return carry
-
-    lax.fori_loop(0, steps, plan_rows, 0, unroll=True)
+    cov_scr[...] = covariance()
 
     smallest = jnp.minimum(jnp.min(low), jnp.min(clow))
     largest = jnp.maximum(jnp.max(high), jnp.max(chigh))
@@ -295,6 +311,7 @@
             return carry
 
         lax.fori_loop(0, n // 16, plan_step, 0)
+        cov_scr[...] = covariance()
 
     own = pl.ds(pl.multiple_of(place * local_rows, local_rows), local_rows)
     f = m_scr[own, :]
@@ -306,14 +323,7 @@
     g = pltpu.roll(g_scr[...], lax.rem(n - place * local_rows, n), 1)
     g_ref[...] = g[:1, :local_rows] * (1.0 / LOG2_SCALE)
 
-    deep = (width + 15) // 16 * 16
-    cov = jnp.zeros((side, side), jnp.float32)
-    for at in range(0, n, chunk):
-        rows = slice(at, at + chunk)
-        hi, lo = split(dot32(p_scr[rows, :], ys))
-        xs_t = xy_scr[rows, :side].T
-        cov = cov + dot32(xs_t, hi) + dot32(xs_t, lo)
-    cov = cov[:deep]
+    cov = cov_scr[...]
     place_y = lax.broadcasted_iota(jnp.int32, (deep, side), 1)
     cov = jnp.where(place_y >= half, cov, 0.0)
     q = cov / jnp.sqrt(jnp.sum(cov * cov))
@@ -369,7 +379,7 @@
             jax.ShapeDtypeStruct((1, local_rows), jnp.float32),
             jax.ShapeDtypeStruct((width, width), jnp.float32),
         ),
-        in_specs=[smem, vmem] + [vmem] * len(masks),
+        in_specs=[smem, vmem] + [pl.BlockSpec(memory_space=pl.ANY)] * len(masks),
         out_specs=(vmem, vmem, vmem),
         scratch_shapes=[
             pltpu.VMEM((n, packed), jnp.bfloat16),
@@ -381,9 +391,10 @@
             pltpu.VMEM((n, LANES), jnp.float32),
             pltpu.VMEM((n, LANES), jnp.float32),
             pltpu.VMEM((8, n), jnp.float32),
-            pltpu.SMEM((1,), jnp.int32),
+            pltpu.VMEM(((width + 15) // 16 * 16, side), jnp.float32),
+            pltpu.SemaphoreType.DMA((len(masks),)),
         ],
-        compiler_params=pltpu.CompilerParams(vmem_limit_bytes=VMEM_BYTES),
+        compiler_params=pltpu.CompilerParams(vmem_limit_bytes=KERNEL_VMEM_BYTES),
         name="transport",
     )(place.reshape(1), mapping, *[held[m] for m in masks])
     return (f.reshape(local_rows), g.reshape(local_rows), rotation)

time: 39.6 us -> 39 us (0.985)
  Pallas kernels: 18.1 us -> 17.1 us
    pallas_call x1, Pallas kernels: 15.7 us -> 14.5 us  [gathered_local(): pl.pallas_call(lambda *refs: transport_kernel(masks, *refs), out_shape=(j...]
    unnamed x30 -> x4, local copies, waits for them, and re-layouts: 0.56 us -> 0.89 us
where the time goes in v3:
time: 39 us; the launch traced here: 38.8 us
  Pallas kernels  17.1 us (44%)
  starting transfers between devices  12.4 us (32%)
  waiting for transfers between devices  7.62 us (20%)
  local copies, waits for them, and re-layouts  0.89 us (2%)
  between operations  0.85 us (2%)
    pallas_call x1, Pallas kernels, gathered_local(): pl.pallas_call(lambda *refs: transport_kernel(masks, *refs), out_shape=(j...  14.5 us
    ppermute x15, starting transfers between devices, swap(): lax.ppermute(a, axis, [(i, i ^ mask) for i in range(lax.axis_size(axis))])  12.4 us
    ppermute x15, waiting for transfers between devices, swap(): lax.ppermute(a, axis, [(i, i ^ mask) for i in range(lax.axis_size(axis))])  7.62 us
    pallas_call x1, Pallas kernels, gathered_local(): pl.pallas_call(pick_kernel, out_shape=jax.ShapeDtypeStruct((local_rows, p...  2.57 us
    unnamed x4, local copies, waits for them, and re-layouts  0.89 us
  transfers between devices with their start and end apart: 15, of which 5 were waited for; matrix products, arithmetic and copies ran while one was open for 0% of the time, Pallas kernels for 0%

profile of v3, /device:TPU:0, one launch (start us, length us, event | category | flops | bytes accessed | tf_op | source)
XLA Modules:
  0.0 38.8 jit_solution(9430927984393644957)
XLA Ops:
  0.7 2.6 %pick_words.1.refs_2_ = bf16[64,640]{1,0:T(8,128)(2,1)} custom-call(s32[1]{0:T(128)} %bitcast.1.base_ref, s32[1,64]{1,0:T(1,128)} %bitcast.10, s32[1,64]{1,0:T(1,128)} %bitcast.11, bf16[300,784]{1,0:T(8,128)(2,1)} %bitcast.8, bf16[300,784]{1,0:T(8,128)(2,1)} %bitcast.9), custom_call_target="tpu_custom_call" | custom-call | tf_op jit(solution)/shard_map/pick_words/pallas_call | solution.py:350
  3.2 5.0 %collective-permute-start.11 = (bf16[64,640]{1,0:T(8,128)(2,1)}, bf16[64,640]{1,0:T(8,128)(2,1)S(1)}, u32[]{:S(2)}, u32[]{:S(2)}) collective-permute-start(bf16[64,640]{1,0:T(8,128)(2,1)} %pick_words.1.refs_2_), channel_id=1, source_target_pairs={{0,12},{4,8},{8,4},{12,0},{1,13},{5,9},{9,5},{13,1},{2,14},{6,10},... | collective-permute-start | bytes 245768 | tf_op jit(solution)/shard_map/ppermute | solution.py:366
  8.3 0.6 %collective-permute-start.3 = (bf16[64,640]{1,0:T(8,128)(2,1)}, bf16[64,640]{1,0:T(8,128)(2,1)S(1)}, u32[]{:S(2)}, u32[]{:S(2)}) collective-permute-start(bf16[64,640]{1,0:T(8,128)(2,1)} %pick_words.1.refs_2_), channel_id=1, source_target_pairs={{0,4},{4,0},{8,12},{12,8},{1,5},{5,1},{9,13},{13,9},{2,6},{6,2},{1... | collective-permute-start | bytes 245768 | tf_op jit(solution)/shard_map/ppermute | solution.py:366
  8.8 1.7 %collective-permute-start.1 = (bf16[64,640]{1,0:T(8,128)(2,1)}, bf16[64,640]{1,0:T(8,128)(2,1)S(1)}, u32[]{:S(2)}, u32[]{:S(2)}) collective-permute-start(bf16[64,640]{1,0:T(8,128)(2,1)} %pick_words.1.refs_2_), channel_id=1, source_target_pairs={{0,2},{2,0},{1,3},{3,1},{4,6},{6,4},{5,7},{7,5},{8,10},{10,8},{9,1... | collective-permute-start | bytes 245768 | tf_op jit(solution)/shard_map/ppermute | solution.py:366
  10.5 0.0 collective-permute-start
  10.6 1.0 %collective-permute-done.11.refs_14_ = bf16[64,640]{1,0:T(8,128)(2,1)S(1)} collective-permute-done((bf16[64,640]{1,0:T(8,128)(2,1)}, bf16[64,640]{1,0:T(8,128)(2,1)S(1)}, u32[]{:S(2)}, u32[]{:S(2)}) %collective-permute-start.11) | collective-permute-done | bytes 81952 | tf_op jit(solution)/shard_map/ppermute | solution.py:366
  11.5 1.8 %collective-permute-start.13 = (bf16[64,640]{1,0:T(8,128)(2,1)S(1)}, bf16[64,640]{1,0:T(8,128)(2,1)S(1)}, u32[]{:S(2)}, u32[]{:S(2)}) collective-permute-start(bf16[64,640]{1,0:T(8,128)(2,1)S(1)} %collective-permute-done.11.refs_14_), channel_id=1, source_target_pairs={{0,2},{2,0},{1,3},{3,1},{4,6},{6,4},{5,7},{7,5},{8,10},{10,8},{9,1... | collective-permute-start | bytes 245768 | tf_op jit(solution)/shard_map/ppermute | solution.py:366
  13.3 2.1 %collective-permute-done.7.refs_10_ = bf16[64,640]{1,0:T(8,128)(2,1)S(1)} collective-permute-done((bf16[64,640]{1,0:T(8,128)(2,1)}, bf16[64,640]{1,0:T(8,128)(2,1)S(1)}, u32[]{:S(2)}, u32[]{:S(2)}) %collective-permute-start.7) | collective-permute-done | bytes 81952 | tf_op jit(solution)/shard_map/ppermute | solution.py:366
  15.3 0.0 collective-permute-start.12
  15.3 0.0 collective-permute-done.3.refs_6_
  15.3 1.5 %collective-permute-start.9 = (bf16[64,640]{1,0:T(8,128)(2,1)S(1)}, bf16[64,640]{1,0:T(8,128)(2,1)S(1)}, u32[]{:S(2)}, u32[]{:S(2)}) collective-permute-start(bf16[64,640]{1,0:T(8,128)(2,1)S(1)} %collective-permute-done.7.refs_10_), channel_id=1, source_target_pairs={{0,2},{2,0},{1,3},{3,1},{4,6},{6,4},{5,7},{7,5},{8,10},{10,8},{9,1... | collective-permute-start | bytes 245768 | tf_op jit(solution)/shard_map/ppermute | solution.py:366
  16.8 0.0 collective-permute-done.1.refs_4_
  16.8 0.2 collective-permute-start.8
  17.1 0.5 %collective-permute-start.5 = (bf16[64,640]{1,0:T(8,128)(2,1)S(1)}, bf16[64,640]{1,0:T(8,128)(2,1)S(1)}, u32[]{:S(2)}, u32[]{:S(2)}) collective-permute-start(bf16[64,640]{1,0:T(8,128)(2,1)S(1)} %collective-permute-done.3.refs_6_), channel_id=1, source_target_pairs={{0,2},{2,0},{1,3},{3,1},{4,6},{6,4},{5,7},{7,5},{8,10},{10,8},{9,1... | collective-permute-start | bytes 245768 | tf_op jit(solution)/shard_map/ppermute | solution.py:366
  17.6 0.0 collective-permute-done.13.refs_16_
  17.6 0.0 collective-permute-start.4
  17.6 0.0 collective-permute-done.12.refs_15_
  17.6 0.5 %collective-permute-start.2 = (bf16[64,640]{1,0:T(8,128)(2,1)S(1)}, bf16[64,640]{1,0:T(8,128)(2,1)S(1)}, u32[]{:S(2)}, u32[]{:S(2)}) collective-permute-start(bf16[64,640]{1,0:T(8,128)(2,1)S(1)} %collective-permute-done.1.refs_4_), channel_id=1, source_target_pairs={{0,1},{1,0},{2,3},{3,2},{4,5},{5,4},{6,7},{7,6},{8,9},{9,8},{10,11... | collective-permute-start | bytes 245768 | tf_op jit(solution)/shard_map/ppermute | solution.py:366
  18.1 2.3 %collective-permute-done.9.refs_12_ = bf16[64,640]{1,0:T(8,128)(2,1)S(1)} collective-permute-done((bf16[64,640]{1,0:T(8,128)(2,1)S(1)}, bf16[64,640]{1,0:T(8,128)(2,1)S(1)}, u32[]{:S(2)}, u32[]{:S(2)}) %collective-permute-start.9) | collective-permute-done | bytes 81952 | tf_op jit(solution)/shard_map/ppermute | solution.py:366
  20.5 0.5 %collective-permute-start.10 = (bf16[64,640]{1,0:T(8,128)(2,1)S(1)}, bf16[64,640]{1,0:T(8,128)(2,1)S(1)}, u32[]{:S(2)}, u32[]{:S(2)}) collective-permute-start(bf16[64,640]{1,0:T(8,128)(2,1)S(1)} %collective-permute-done.9.refs_12_), channel_id=1, source_target_pairs={{0,1},{1,0},{2,3},{3,2},{4,5},{5,4},{6,7},{7,6},{8,9},{9,8},{10,11... | collective-permute-start | bytes 245768 | tf_op jit(solution)/shard_map/ppermute | solution.py:366
  21.0 1.0 %collective-permute-done.5.refs_8_ = bf16[64,640]{1,0:T(8,128)(2,1)S(1)} collective-permute-done((bf16[64,640]{1,0:T(8,128)(2,1)S(1)}, bf16[64,640]{1,0:T(8,128)(2,1)S(1)}, u32[]{:S(2)}, u32[]{:S(2)}) %collective-permute-start.5) | collective-permute-done | bytes 81952 | tf_op jit(solution)/shard_map/ppermute | solution.py:366
  22.0 1.2 %collective-permute-done.6.refs_9_ = bf16[64,640]{1,0:T(8,128)(2,1)S(1)} collective-permute-done((bf16[64,640]{1,0:T(8,128)(2,1)S(1)}, bf16[64,640]{1,0:T(8,128)(2,1)S(1)}, u32[]{:S(2)}, u32[]{:S(2)}) %collective-permute-start.6) | collective-permute-done | bytes 81952 | tf_op jit(solution)/shard_map/ppermute | solution.py:366
  23.2 0.9 %copy-done.1 = bf16[64,640]{1,0:T(8,128)(2,1)S(1)} copy-done((bf16[64,640]{1,0:T(8,128)(2,1)S(1)}, bf16[64,640]{1,0:T(8,128)(2,1)}, u32[]{:S(2)}) %copy-start.1) | copy-done | bytes 81944
  24.1 14.5 %transport.1 = (f32[1,64]{1,0:T(1,128)}, f32[1,64]{1,0:T(1,128)}, f32[300,300]{1,0:T(8,128)}) custom-call(s32[1]{0:T(128)} %bitcast.refs_0_, f32[300,300]{1,0:T(8,128)S(1)} %copy-done, bf16[64,640]{1,0:T(8,128)(2,1)S(1)} %copy-done.1, bf16[64,640]{1,0:T(8,128)(2,1)S(1)} %collective-permute-done.refs_3_, bf16[64,640]{1,0:T(8,128)(2,1)S(1)} %collective-permute-done.1.refs_4_, ...), custom_call_target="tpu_custom_call" | custom-call | tf_op jit(solution)/shard_map/transport/pallas_call | solution.py:375
  (12 shorter events, 0.0 us)
Async XLA Ops:
  0.6 22.6 %copy-start = (f32[300,300]{1,0:T(8,128)S(1)}, f32[300,300]{1,0:T(8,128)}, u32[]{:S(2)}) copy-start(f32[300,300]{1,0:T(8,128)} %refs_1_.1) | copy-start | bytes 1080004
  3.2 8.3 %collective-permute-start.11 = (bf16[64,640]{1,0:T(8,128)(2,1)}, bf16[64,640]{1,0:T(8,128)(2,1)S(1)}, u32[]{:S(2)}, u32[]{:S(2)}) collective-permute-start(bf16[64,640]{1,0:T(8,128)(2,1)} %pick_words.1.refs_2_), channel_id=1, source_target_pairs={{0,12},{4,8},{8,4},{12,0},{1,13},{5,9},{9,5},{13,1},{2,14},{6,10},... | collective-permute-start | bytes 245768 | tf_op jit(solution)/shard_map/ppermute | solution.py:366
  8.3 7.1 %collective-permute-start.7 = (bf16[64,640]{1,0:T(8,128)(2,1)}, bf16[64,640]{1,0:T(8,128)(2,1)S(1)}, u32[]{:S(2)}, u32[]{:S(2)}) collective-permute-start(bf16[64,640]{1,0:T(8,128)(2,1)} %pick_words.1.refs_2_), channel_id=1, source_target_pairs={{0,8},{4,12},{8,0},{12,4},{1,9},{5,13},{9,1},{13,5},{2,10},{6,14},... | collective-permute-start | bytes 245768 | tf_op jit(solution)/shard_map/ppermute | solution.py:366
  8.3 7.1 %collective-permute-start.3 = (bf16[64,640]{1,0:T(8,128)(2,1)}, bf16[64,640]{1,0:T(8,128)(2,1)S(1)}, u32[]{:S(2)}, u32[]{:S(2)}) collective-permute-start(bf16[64,640]{1,0:T(8,128)(2,1)} %pick_words.1.refs_2_), channel_id=1, source_target_pairs={{0,4},{4,0},{8,12},{12,8},{1,5},{5,1},{9,13},{13,9},{2,6},{6,2},{1... | collective-permute-start | bytes 245768 | tf_op jit(solution)/shard_map/ppermute | solution.py:366
  8.8 8.0 %collective-permute-start.1 = (bf16[64,640]{1,0:T(8,128)(2,1)}, bf16[64,640]{1,0:T(8,128)(2,1)S(1)}, u32[]{:S(2)}, u32[]{:S(2)}) collective-permute-start(bf16[64,640]{1,0:T(8,128)(2,1)} %pick_words.1.refs_2_), channel_id=1, source_target_pairs={{0,2},{2,0},{1,3},{3,1},{4,6},{6,4},{5,7},{7,5},{8,10},{10,8},{9,1... | collective-permute-start | bytes 245768 | tf_op jit(solution)/shard_map/ppermute | solution.py:366
  10.5 6.5 %collective-permute-start = (bf16[64,640]{1,0:T(8,128)(2,1)}, bf16[64,640]{1,0:T(8,128)(2,1)S(1)}, u32[]{:S(2)}, u32[]{:S(2)}) collective-permute-start(bf16[64,640]{1,0:T(8,128)(2,1)} %pick_words.1.refs_2_), channel_id=1, source_target_pairs={{0,1},{1,0},{2,3},{3,2},{4,5},{5,4},{6,7},{7,6},{8,9},{9,8},{10,11... | collective-permute-start | bytes 245768 | tf_op jit(solution)/shard_map/ppermute | solution.py:366
  11.5 6.1 %collective-permute-start.13 = (bf16[64,640]{1,0:T(8,128)(2,1)S(1)}, bf16[64,640]{1,0:T(8,128)(2,1)S(1)}, u32[]{:S(2)}, u32[]{:S(2)}) collective-permute-start(bf16[64,640]{1,0:T(8,128)(2,1)S(1)} %collective-permute-done.11.refs_14_), channel_id=1, source_target_pairs={{0,2},{2,0},{1,3},{3,1},{4,6},{6,4},{5,7},{7,5},{8,10},{10,8},{9,1... | collective-permute-start | bytes 245768 | tf_op jit(solution)/shard_map/ppermute | solution.py:366
  15.3 2.3 %collective-permute-start.12 = (bf16[64,640]{1,0:T(8,128)(2,1)S(1)}, bf16[64,640]{1,0:T(8,128)(2,1)S(1)}, u32[]{:S(2)}, u32[]{:S(2)}) collective-permute-start(bf16[64,640]{1,0:T(8,128)(2,1)S(1)} %collective-permute-done.11.refs_14_), channel_id=1, source_target_pairs={{0,1},{1,0},{2,3},{3,2},{4,5},{5,4},{6,7},{7,6},{8,9},{9,8},{10,11... | collective-permute-start | bytes 245768 | tf_op jit(solution)/shard_map/ppermute | solution.py:366
  15.3 5.1 %collective-permute-start.9 = (bf16[64,640]{1,0:T(8,128)(2,1)S(1)}, bf16[64,640]{1,0:T(8,128)(2,1)S(1)}, u32[]{:S(2)}, u32[]{:S(2)}) collective-permute-start(bf16[64,640]{1,0:T(8,128)(2,1)S(1)} %collective-permute-done.7.refs_10_), channel_id=1, source_target_pairs={{0,2},{2,0},{1,3},{3,1},{4,6},{6,4},{5,7},{7,5},{8,10},{10,8},{9,1... | collective-permute-start | bytes 245768 | tf_op jit(solution)/shard_map/ppermute | solution.py:366
  16.8 3.6 %collective-permute-start.8 = (bf16[64,640]{1,0:T(8,128)(2,1)S(1)}, bf16[64,640]{1,0:T(8,128)(2,1)S(1)}, u32[]{:S(2)}, u32[]{:S(2)}) collective-permute-start(bf16[64,640]{1,0:T(8,128)(2,1)S(1)} %collective-permute-done.7.refs_10_), channel_id=1, source_target_pairs={{0,1},{1,0},{2,3},{3,2},{4,5},{5,4},{6,7},{7,6},{8,9},{9,8},{10,11... | collective-permute-start | bytes 245768 | tf_op jit(solution)/shard_map/ppermute | solution.py:366
  17.1 4.9 %collective-permute-start.5 = (bf16[64,640]{1,0:T(8,128)(2,1)S(1)}, bf16[64,640]{1,0:T(8,128)(2,1)S(1)}, u32[]{:S(2)}, u32[]{:S(2)}) collective-permute-start(bf16[64,640]{1,0:T(8,128)(2,1)S(1)} %collective-permute-done.3.refs_6_), channel_id=1, source_target_pairs={{0,2},{2,0},{1,3},{3,1},{4,6},{6,4},{5,7},{7,5},{8,10},{10,8},{9,1... | collective-permute-start | bytes 245768 | tf_op jit(solution)/shard_map/ppermute | solution.py:366
  17.6 4.4 %collective-permute-start.4 = (bf16[64,640]{1,0:T(8,128)(2,1)S(1)}, bf16[64,640]{1,0:T(8,128)(2,1)S(1)}, u32[]{:S(2)}, u32[]{:S(2)}) collective-permute-start(bf16[64,640]{1,0:T(8,128)(2,1)S(1)} %collective-permute-done.3.refs_6_), channel_id=1, source_target_pairs={{0,1},{1,0},{2,3},{3,2},{4,5},{5,4},{6,7},{7,6},{8,9},{9,8},{10,11... | collective-permute-start | bytes 245768 | tf_op jit(solution)/shard_map/ppermute | solution.py:366
  17.6 4.3 %collective-permute-start.2 = (bf16[64,640]{1,0:T(8,128)(2,1)S(1)}, bf16[64,640]{1,0:T(8,128)(2,1)S(1)}, u32[]{:S(2)}, u32[]{:S(2)}) collective-permute-start(bf16[64,640]{1,0:T(8,128)(2,1)S(1)} %collective-permute-done.1.refs_4_), channel_id=1, source_target_pairs={{0,1},{1,0},{2,3},{3,2},{4,5},{5,4},{6,7},{7,6},{8,9},{9,8},{10,11... | collective-permute-start | bytes 245768 | tf_op jit(solution)/shard_map/ppermute | solution.py:366
  20.4 1.5 %collective-permute-start.14 = (bf16[64,640]{1,0:T(8,128)(2,1)S(1)}, bf16[64,640]{1,0:T(8,128)(2,1)S(1)}, u32[]{:S(2)}, u32[]{:S(2)}) collective-permute-start(bf16[64,640]{1,0:T(8,128)(2,1)S(1)} %collective-permute-done.13.refs_16_), channel_id=1, source_target_pairs={{0,1},{1,0},{2,3},{3,2},{4,5},{5,4},{6,7},{7,6},{8,9},{9,8},{10,11... | collective-permute-start | bytes 245768 | tf_op jit(solution)/shard_map/ppermute | solution.py:366
  20.5 1.5 %collective-permute-start.10 = (bf16[64,640]{1,0:T(8,128)(2,1)S(1)}, bf16[64,640]{1,0:T(8,128)(2,1)S(1)}, u32[]{:S(2)}, u32[]{:S(2)}) collective-permute-start(bf16[64,640]{1,0:T(8,128)(2,1)S(1)} %collective-permute-done.9.refs_12_), channel_id=1, source_target_pairs={{0,1},{1,0},{2,3},{3,2},{4,5},{5,4},{6,7},{7,6},{8,9},{9,8},{10,11... | collective-permute-start | bytes 245768 | tf_op jit(solution)/shard_map/ppermute | solution.py:366
  22.0 1.3 %collective-permute-start.6 = (bf16[64,640]{1,0:T(8,128)(2,1)S(1)}, bf16[64,640]{1,0:T(8,128)(2,1)S(1)}, u32[]{:S(2)}, u32[]{:S(2)}) collective-permute-start(bf16[64,640]{1,0:T(8,128)(2,1)S(1)} %collective-permute-done.5.refs_8_), channel_id=1, source_target_pairs={{0,1},{1,0},{2,3},{3,2},{4,5},{5,4},{6,7},{7,6},{8,9},{9,8},{10,11... | collective-permute-start | bytes 245768 | tf_op jit(solution)/shard_map/ppermute | solution.py:366
  23.2 0.9 %copy-start.1 = (bf16[64,640]{1,0:T(8,128)(2,1)S(1)}, bf16[64,640]{1,0:T(8,128)(2,1)}, u32[]{:S(2)}) copy-start(bf16[64,640]{1,0:T(8,128)(2,1)} %pick_words.1.refs_2_) | copy-start | bytes 245764

commit v4 on v3

--- a/solution.py
+++ b/solution.py
@@ -121,15 +121,29 @@
     out_ref[:, head + LANES :] = target[:, :head]
 
 
-def transport_kernel(masks, place_ref, mapping_ref, *refs):
+def map_kernel(mapping_ref, out_ref):
+    width = mapping_ref.shape[0]
+    head = width // LANES * LANES
+    half = LANES // 2
+    tail = width - head
+    out_ref[...] = jnp.zeros_like(out_ref)
+    for at, part in enumerate(split(mapping_ref[...])):
+        top, low = head * at, head * 2 + LANES * at
+        for row, rows in ((top, part[:head]), (low, part[head:])):
+            count = rows.shape[0]
+            out_ref[row : row + count, half : half + tail] = rows[:, head:]
+            out_ref[row : row + count, LANES:] = rows[:, :head]
+
+
+def transport_kernel(masks, place_ref, map_ref, *refs):
     blocks = refs[: len(masks)]
     f_ref, g_ref, rot_ref = refs[len(masks) : len(masks) + 3]
-    xy_scr, map_hi, map_lo, xw_scr, k_scr, p_scr, m_scr, u_scr, g_scr, cov_scr, sems = refs[
+    xy_scr, xw_scr, k_scr, p_scr, m_scr, u_scr, g_scr, cov_scr, sems = refs[
         len(masks) + 3 :
     ]
     local_rows = blocks[0].shape[0]
     n = xy_scr.shape[0]
-    width = mapping_ref.shape[0]
+    width = rot_ref.shape[0]
     head = width // LANES * LANES
     tail = width - head
     side = head + LANES
@@ -147,12 +161,6 @@
             pltpu.make_async_copy(block, xy_scr.at[pl.ds(row, local_rows), :], sems.at[at])
         )
         copies[-1].start()
-
-    hi, lo = split(mapping_ref[...])
-    for scr, part in ((map_hi, hi), (map_lo, lo)):
-        scr[...] = jnp.zeros_like(scr)
-        scr[:width, half : half + tail] = part[:, head:]
-        scr[:width, LANES:] = part[:, :head]
 
     for copy in copies:
         copy.wait()
@@ -201,7 +209,7 @@
 
     steps = n // step_rows
     carry = (zeros, inf8, -inf8)
-    map_all = jnp.concatenate([map_hi[:head], map_lo[:head], map_hi[head:], map_lo[head:]], axis=0)
+    map_all = map_ref[...]
     for at in range(0, n, chunk):
         rows = slice(at, at + chunk)
         xs = xy_scr[rows, :side]
@@ -371,6 +379,16 @@
             for key in [k for k in held if (k // below) % lax.axis_size(axis) == 0]:
                 held[key + mask * below] = swap(held[key], axis, mask)
     masks = sorted(held)
+    middle = masks[min(len(masks) // 2 + sizes[2], len(masks) - 1)]
+    mapping, held[middle] = lax.optimization_barrier((mapping, held[middle]))
+    halves = pl.pallas_call(
+        map_kernel,
+        out_shape=jax.ShapeDtypeStruct((2 * side, side), jnp.bfloat16),
+        in_specs=[vmem],
+        out_specs=vmem,
+        compiler_params=pltpu.CompilerParams(vmem_limit_bytes=4 * 1024 * 1024),
+        name="map_halves",
+    )(mapping)
     n = local_rows * len(masks)
     f, g, rotation = pl.pallas_call(
         lambda *refs: transport_kernel(masks, *refs),
@@ -383,8 +401,6 @@
         out_specs=(vmem, vmem, vmem),
         scratch_shapes=[
             pltpu.VMEM((n, packed), jnp.bfloat16),
-            pltpu.VMEM((side, side), jnp.bfloat16),
-            pltpu.VMEM((side, side), jnp.bfloat16),
             pltpu.VMEM((n, side), jnp.bfloat16),
             pltpu.VMEM((n, n), jnp.float32),
             pltpu.VMEM((n, n), jnp.bfloat16),
@@ -396,7 +412,7 @@
         ],
         compiler_params=pltpu.CompilerParams(vmem_limit_bytes=KERNEL_VMEM_BYTES),
         name="transport",
-    )(place.reshape(1), mapping, *[held[m] for m in masks])
+    )(place.reshape(1), halves, *[held[m] for m in masks])
     return (f.reshape(local_rows), g.reshape(local_rows), rotation)
 
 

time: 39 us -> 37.9 us (0.972)
  local copies, waits for them, and re-layouts: 0.89 us -> 0.01 us
  starting transfers between devices: 12.4 us -> 11.9 us
    unnamed x4, local copies, waits for them, and re-layouts: 0.89 us -> 0.01 us
    ppermute x15, starting transfers between devices: 12.4 us -> 11.9 us  [swap(): lax.ppermute(a, axis, [(i, i ^ mask) for i in range(lax.axis_size(axis))])]
where the time goes in v4:
time: 37.9 us; the launch traced here: 37.7 us
  Pallas kernels  17.1 us (45%)
  starting transfers between devices  11.9 us (31%)
  waiting for transfers between devices  7.9 us (21%)
  between operations  0.86 us (2%)
    pallas_call x1, Pallas kernels, gathered_local(): pl.pallas_call(lambda *refs: transport_kernel(masks, *refs), out_shape=(j...  14.4 us
    ppermute x15, starting transfers between devices, swap(): lax.ppermute(a, axis, [(i, i ^ mask) for i in range(lax.axis_size(axis))])  11.9 us
    ppermute x15, waiting for transfers between devices, swap(): lax.ppermute(a, axis, [(i, i ^ mask) for i in range(lax.axis_size(axis))])  7.9 us
    pallas_call x1, Pallas kernels, gathered_local(): pl.pallas_call(pick_kernel, out_shape=jax.ShapeDtypeStruct((local_rows, p...  2.57 us
  transfers between devices with their start and end apart: 15, of which 5 were waited for; matrix products, arithmetic and copies ran while one was open for 0% of the time, Pallas kernels for 0%

profile of v4, /device:TPU:0, one launch (start us, length us, event | category | flops | bytes accessed | tf_op | source)
XLA Modules:
  0.0 37.7 jit_solution(3563947001459219920)
XLA Ops:
  0.7 2.6 %pick_words.1.refs_2_ = bf16[64,640]{1,0:T(8,128)(2,1)} custom-call(s32[1]{0:T(128)} %bitcast.1.base_ref, s32[1,64]{1,0:T(1,128)} %bitcast.10, s32[1,64]{1,0:T(1,128)} %bitcast.11, bf16[300,784]{1,0:T(8,128)(2,1)} %bitcast.8, bf16[300,784]{1,0:T(8,128)(2,1)} %bitcast.9), custom_call_target="tpu_custom_call" | custom-call | tf_op jit(solution)/shard_map/pick_words/pallas_call | solution.py:358
  3.2 5.0 %collective-permute-start.11 = (bf16[64,640]{1,0:T(8,128)(2,1)}, bf16[64,640]{1,0:T(8,128)(2,1)S(1)}, u32[]{:S(2)}, u32[]{:S(2)}) collective-permute-start(bf16[64,640]{1,0:T(8,128)(2,1)} %pick_words.1.refs_2_), channel_id=1, source_target_pairs={{0,12},{4,8},{8,4},{12,0},{1,13},{5,9},{9,5},{13,1},{2,14},{6,10},... | collective-permute-start | bytes 245768 | tf_op jit(solution)/shard_map/ppermute | solution.py:374
  8.3 1.5 %collective-permute-start.3 = (bf16[64,640]{1,0:T(8,128)(2,1)}, bf16[64,640]{1,0:T(8,128)(2,1)S(1)}, u32[]{:S(2)}, u32[]{:S(2)}) collective-permute-start(bf16[64,640]{1,0:T(8,128)(2,1)} %pick_words.1.refs_2_), channel_id=1, source_target_pairs={{0,2},{2,0},{1,3},{3,1},{4,6},{6,4},{5,7},{7,5},{8,10},{10,8},{9,1... | collective-permute-start | bytes 245768 | tf_op jit(solution)/shard_map/ppermute | solution.py:374
  9.8 0.0 collective-permute-start.2
  9.8 0.8 %collective-permute-start = (bf16[64,640]{1,0:T(8,128)(2,1)}, bf16[64,640]{1,0:T(8,128)(2,1)S(1)}, u32[]{:S(2)}, u32[]{:S(2)}) collective-permute-start(bf16[64,640]{1,0:T(8,128)(2,1)} %pick_words.1.refs_2_), channel_id=1, source_target_pairs={{0,8},{4,12},{8,0},{12,4},{1,9},{5,13},{9,1},{13,5},{2,10},{6,14},... | collective-permute-start | bytes 245768 | tf_op jit(solution)/shard_map/ppermute | solution.py:374
  10.6 1.3 %collective-permute-done.11.refs_14_ = bf16[64,640]{1,0:T(8,128)(2,1)S(1)} collective-permute-done((bf16[64,640]{1,0:T(8,128)(2,1)}, bf16[64,640]{1,0:T(8,128)(2,1)S(1)}, u32[]{:S(2)}, u32[]{:S(2)}) %collective-permute-start.11) | collective-permute-done | bytes 81952 | tf_op jit(solution)/shard_map/ppermute | solution.py:374
  11.8 1.6 %collective-permute-start.13 = (bf16[64,640]{1,0:T(8,128)(2,1)S(1)}, bf16[64,640]{1,0:T(8,128)(2,1)S(1)}, u32[]{:S(2)}, u32[]{:S(2)}) collective-permute-start(bf16[64,640]{1,0:T(8,128)(2,1)S(1)} %collective-permute-done.11.refs_14_), channel_id=1, source_target_pairs={{0,2},{2,0},{1,3},{3,1},{4,6},{6,4},{5,7},{7,5},{8,10},{10,8},{9,1... | collective-permute-start | bytes 245768 | tf_op jit(solution)/shard_map/ppermute | solution.py:374
  13.5 0.0 collective-permute-done.5.refs_6_
  13.5 0.0 collective-permute-start.12
  13.5 0.0 collective-permute-done.3.refs_4_
  13.5 1.3 %collective-permute-start.7 = (bf16[64,640]{1,0:T(8,128)(2,1)S(1)}, bf16[64,640]{1,0:T(8,128)(2,1)S(1)}, u32[]{:S(2)}, u32[]{:S(2)}) collective-permute-start(bf16[64,640]{1,0:T(8,128)(2,1)S(1)} %collective-permute-done.5.refs_6_), channel_id=1, source_target_pairs={{0,2},{2,0},{1,3},{3,1},{4,6},{6,4},{5,7},{7,5},{8,10},{10,8},{9,1... | collective-permute-start | bytes 245768 | tf_op jit(solution)/shard_map/ppermute | solution.py:374
  14.8 0.0 collective-permute-done.2.refs_3_
  14.8 0.0 collective-permute-start.6
  14.8 2.7 %collective-permute-done.refs_10_ = bf16[64,640]{1,0:T(8,128)(2,1)S(1)} collective-permute-done((bf16[64,640]{1,0:T(8,128)(2,1)}, bf16[64,640]{1,0:T(8,128)(2,1)S(1)}, u32[]{:S(2)}, u32[]{:S(2)}) %collective-permute-start) | collective-permute-done | bytes 81952 | tf_op jit(solution)/shard_map/ppermute | solution.py:374
  17.5 0.5 %collective-permute-start.1 = (bf16[64,640]{1,0:T(8,128)(2,1)S(1)}, bf16[64,640]{1,0:T(8,128)(2,1)S(1)}, u32[]{:S(2)}, u32[]{:S(2)}) collective-permute-start(bf16[64,640]{1,0:T(8,128)(2,1)S(1)} %collective-permute-done.refs_10_), channel_id=1, source_target_pairs={{0,2},{2,0},{1,3},{3,1},{4,6},{6,4},{5,7},{7,5},{8,10},{10,8},{9,1... | collective-permute-start | bytes 245768 | tf_op jit(solution)/shard_map/ppermute | solution.py:374
  18.0 0.0 collective-permute-done.13.refs_16_
  18.0 0.5 %collective-permute-start.4 = (bf16[64,640]{1,0:T(8,128)(2,1)S(1)}, bf16[64,640]{1,0:T(8,128)(2,1)S(1)}, u32[]{:S(2)}, u32[]{:S(2)}) collective-permute-start(bf16[64,640]{1,0:T(8,128)(2,1)S(1)} %collective-permute-done.3.refs_4_), channel_id=1, source_target_pairs={{0,1},{1,0},{2,3},{3,2},{4,5},{5,4},{6,7},{7,6},{8,9},{9,8},{10,11... | collective-permute-start | bytes 245768 | tf_op jit(solution)/shard_map/ppermute | solution.py:374
  18.5 0.1 collective-permute-done.7.refs_8_
  18.6 0.5 %collective-permute-start.8 = (bf16[64,640]{1,0:T(8,128)(2,1)S(1)}, bf16[64,640]{1,0:T(8,128)(2,1)S(1)}, u32[]{:S(2)}, u32[]{:S(2)}) collective-permute-start(bf16[64,640]{1,0:T(8,128)(2,1)S(1)} %collective-permute-done.7.refs_8_), channel_id=1, source_target_pairs={{0,1},{1,0},{2,3},{3,2},{4,5},{5,4},{6,7},{7,6},{8,9},{9,8},{10,11... | collective-permute-start | bytes 245768 | tf_op jit(solution)/shard_map/ppermute | solution.py:374
  19.1 2.8 %collective-permute-done.1.refs_12_ = bf16[64,640]{1,0:T(8,128)(2,1)S(1)} collective-permute-done((bf16[64,640]{1,0:T(8,128)(2,1)S(1)}, bf16[64,640]{1,0:T(8,128)(2,1)S(1)}, u32[]{:S(2)}, u32[]{:S(2)}) %collective-permute-start.1) | collective-permute-done | bytes 81952 | tf_op jit(solution)/shard_map/ppermute | solution.py:374
  21.9 0.0 collective-permute-start.10
  21.9 0.2 map_halves.1.refs_1_
  22.2 1.0 %collective-permute-done.10.refs_13_ = bf16[64,640]{1,0:T(8,128)(2,1)S(1)} collective-permute-done((bf16[64,640]{1,0:T(8,128)(2,1)S(1)}, bf16[64,640]{1,0:T(8,128)(2,1)S(1)}, u32[]{:S(2)}, u32[]{:S(2)}) %collective-permute-start.10) | collective-permute-done | bytes 81952 | tf_op jit(solution)/shard_map/ppermute | solution.py:374
  23.2 14.4 %transport.1 = (f32[1,64]{1,0:T(1,128)}, f32[1,64]{1,0:T(1,128)}, f32[300,300]{1,0:T(8,128)}) custom-call(s32[1]{0:T(128)} %bitcast.refs_0_, bf16[768,384]{1,0:T(8,128)(2,1)S(1)} %map_halves.1.refs_1_, bf16[64,640]{1,0:T(8,128)(2,1)S(1)} %copy-done.1, bf16[64,640]{1,0:T(8,128)(2,1)S(1)} %collective-permute-done.2.refs_3_, ...), custom_call_target="tpu_custom_call" | custom-call | tf_op jit(solution)/shard_map/transport/pallas_call | solution.py:393
  (13 shorter events, 0.0 us)
Async XLA Ops:
  0.6 21.3 %copy-start = (f32[300,300]{1,0:T(8,128)S(1)}, f32[300,300]{1,0:T(8,128)}, u32[]{:S(2)}) copy-start(f32[300,300]{1,0:T(8,128)} %mapping_ref) | copy-start | bytes 1080004
  3.2 20.0 %copy-start.1 = (bf16[64,640]{1,0:T(8,128)(2,1)S(1)}, bf16[64,640]{1,0:T(8,128)(2,1)}, u32[]{:S(2)}) copy-start(bf16[64,640]{1,0:T(8,128)(2,1)} %pick_words.1.refs_2_) | copy-start | bytes 245764
  3.2 8.6 %collective-permute-start.11 = (bf16[64,640]{1,0:T(8,128)(2,1)}, bf16[64,640]{1,0:T(8,128)(2,1)S(1)}, u32[]{:S(2)}, u32[]{:S(2)}) collective-permute-start(bf16[64,640]{1,0:T(8,128)(2,1)} %pick_words.1.refs_2_), channel_id=1, source_target_pairs={{0,12},{4,8},{8,4},{12,0},{1,13},{5,9},{9,5},{13,1},{2,14},{6,10},... | collective-permute-start | bytes 245768 | tf_op jit(solution)/shard_map/ppermute | solution.py:374
  8.3 5.2 %collective-permute-start.5 = (bf16[64,640]{1,0:T(8,128)(2,1)}, bf16[64,640]{1,0:T(8,128)(2,1)S(1)}, u32[]{:S(2)}, u32[]{:S(2)}) collective-permute-start(bf16[64,640]{1,0:T(8,128)(2,1)} %pick_words.1.refs_2_), channel_id=1, source_target_pairs={{0,4},{4,0},{8,12},{12,8},{1,5},{5,1},{9,13},{13,9},{2,6},{6,2},{1... | collective-permute-start | bytes 245768 | tf_op jit(solution)/shard_map/ppermute | solution.py:374
  8.3 5.2 %collective-permute-start.3 = (bf16[64,640]{1,0:T(8,128)(2,1)}, bf16[64,640]{1,0:T(8,128)(2,1)S(1)}, u32[]{:S(2)}, u32[]{:S(2)}) collective-permute-start(bf16[64,640]{1,0:T(8,128)(2,1)} %pick_words.1.refs_2_), channel_id=1, source_target_pairs={{0,2},{2,0},{1,3},{3,1},{4,6},{6,4},{5,7},{7,5},{8,10},{10,8},{9,1... | collective-permute-start | bytes 245768 | tf_op jit(solution)/shard_map/ppermute | solution.py:374
  9.8 5.0 %collective-permute-start.2 = (bf16[64,640]{1,0:T(8,128)(2,1)}, bf16[64,640]{1,0:T(8,128)(2,1)S(1)}, u32[]{:S(2)}, u32[]{:S(2)}) collective-permute-start(bf16[64,640]{1,0:T(8,128)(2,1)} %pick_words.1.refs_2_), channel_id=1, source_target_pairs={{0,1},{1,0},{2,3},{3,2},{4,5},{5,4},{6,7},{7,6},{8,9},{9,8},{10,11... | collective-permute-start | bytes 245768 | tf_op jit(solution)/shard_map/ppermute | solution.py:374
  9.8 7.7 %collective-permute-start = (bf16[64,640]{1,0:T(8,128)(2,1)}, bf16[64,640]{1,0:T(8,128)(2,1)S(1)}, u32[]{:S(2)}, u32[]{:S(2)}) collective-permute-start(bf16[64,640]{1,0:T(8,128)(2,1)} %pick_words.1.refs_2_), channel_id=1, source_target_pairs={{0,8},{4,12},{8,0},{12,4},{1,9},{5,13},{9,1},{13,5},{2,10},{6,14},... | collective-permute-start | bytes 245768 | tf_op jit(solution)/shard_map/ppermute | solution.py:374
  11.8 6.2 %collective-permute-start.13 = (bf16[64,640]{1,0:T(8,128)(2,1)S(1)}, bf16[64,640]{1,0:T(8,128)(2,1)S(1)}, u32[]{:S(2)}, u32[]{:S(2)}) collective-permute-start(bf16[64,640]{1,0:T(8,128)(2,1)S(1)} %collective-permute-done.11.refs_14_), channel_id=1, source_target_pairs={{0,2},{2,0},{1,3},{3,1},{4,6},{6,4},{5,7},{7,5},{8,10},{10,8},{9,1... | collective-permute-start | bytes 245768 | tf_op jit(solution)/shard_map/ppermute | solution.py:374
  13.5 4.6 %collective-permute-start.12 = (bf16[64,640]{1,0:T(8,128)(2,1)S(1)}, bf16[64,640]{1,0:T(8,128)(2,1)S(1)}, u32[]{:S(2)}, u32[]{:S(2)}) collective-permute-start(bf16[64,640]{1,0:T(8,128)(2,1)S(1)} %collective-permute-done.11.refs_14_), channel_id=1, source_target_pairs={{0,1},{1,0},{2,3},{3,2},{4,5},{5,4},{6,7},{7,6},{8,9},{9,8},{10,11... | collective-permute-start | bytes 245768 | tf_op jit(solution)/shard_map/ppermute | solution.py:374
  13.5 5.1 %collective-permute-start.7 = (bf16[64,640]{1,0:T(8,128)(2,1)S(1)}, bf16[64,640]{1,0:T(8,128)(2,1)S(1)}, u32[]{:S(2)}, u32[]{:S(2)}) collective-permute-start(bf16[64,640]{1,0:T(8,128)(2,1)S(1)} %collective-permute-done.5.refs_6_), channel_id=1, source_target_pairs={{0,2},{2,0},{1,3},{3,1},{4,6},{6,4},{5,7},{7,5},{8,10},{10,8},{9,1... | collective-permute-start | bytes 245768 | tf_op jit(solution)/shard_map/ppermute | solution.py:374
  14.8 3.8 %collective-permute-start.6 = (bf16[64,640]{1,0:T(8,128)(2,1)S(1)}, bf16[64,640]{1,0:T(8,128)(2,1)S(1)}, u32[]{:S(2)}, u32[]{:S(2)}) collective-permute-start(bf16[64,640]{1,0:T(8,128)(2,1)S(1)} %collective-permute-done.5.refs_6_), channel_id=1, source_target_pairs={{0,1},{1,0},{2,3},{3,2},{4,5},{5,4},{6,7},{7,6},{8,9},{9,8},{10,11... | collective-permute-start | bytes 245768 | tf_op jit(solution)/shard_map/ppermute | solution.py:374
  17.5 4.4 %collective-permute-start.1 = (bf16[64,640]{1,0:T(8,128)(2,1)S(1)}, bf16[64,640]{1,0:T(8,128)(2,1)S(1)}, u32[]{:S(2)}, u32[]{:S(2)}) collective-permute-start(bf16[64,640]{1,0:T(8,128)(2,1)S(1)} %collective-permute-done.refs_10_), channel_id=1, source_target_pairs={{0,2},{2,0},{1,3},{3,1},{4,6},{6,4},{5,7},{7,5},{8,10},{10,8},{9,1... | collective-permute-start | bytes 245768 | tf_op jit(solution)/shard_map/ppermute | solution.py:374
  18.0 4.1 %collective-permute-start.9 = (bf16[64,640]{1,0:T(8,128)(2,1)S(1)}, bf16[64,640]{1,0:T(8,128)(2,1)S(1)}, u32[]{:S(2)}, u32[]{:S(2)}) collective-permute-start(bf16[64,640]{1,0:T(8,128)(2,1)S(1)} %collective-permute-done.refs_10_), channel_id=1, source_target_pairs={{0,1},{1,0},{2,3},{3,2},{4,5},{5,4},{6,7},{7,6},{8,9},{9,8},{10,11... | collective-permute-start | bytes 245768 | tf_op jit(solution)/shard_map/ppermute | solution.py:374
  18.0 4.1 %collective-permute-start.4 = (bf16[64,640]{1,0:T(8,128)(2,1)S(1)}, bf16[64,640]{1,0:T(8,128)(2,1)S(1)}, u32[]{:S(2)}, u32[]{:S(2)}) collective-permute-start(bf16[64,640]{1,0:T(8,128)(2,1)S(1)} %collective-permute-done.3.refs_4_), channel_id=1, source_target_pairs={{0,1},{1,0},{2,3},{3,2},{4,5},{5,4},{6,7},{7,6},{8,9},{9,8},{10,11... | collective-permute-start | bytes 245768 | tf_op jit(solution)/shard_map/ppermute | solution.py:374
  18.6 3.5 %collective-permute-start.14 = (bf16[64,640]{1,0:T(8,128)(2,1)S(1)}, bf16[64,640]{1,0:T(8,128)(2,1)S(1)}, u32[]{:S(2)}, u32[]{:S(2)}) collective-permute-start(bf16[64,640]{1,0:T(8,128)(2,1)S(1)} %collective-permute-done.13.refs_16_), channel_id=1, source_target_pairs={{0,1},{1,0},{2,3},{3,2},{4,5},{5,4},{6,7},{7,6},{8,9},{9,8},{10,11... | collective-permute-start | bytes 245768 | tf_op jit(solution)/shard_map/ppermute | solution.py:374
  18.6 3.5 %collective-permute-start.8 = (bf16[64,640]{1,0:T(8,128)(2,1)S(1)}, bf16[64,640]{1,0:T(8,128)(2,1)S(1)}, u32[]{:S(2)}, u32[]{:S(2)}) collective-permute-start(bf16[64,640]{1,0:T(8,128)(2,1)S(1)} %collective-permute-done.7.refs_8_), channel_id=1, source_target_pairs={{0,1},{1,0},{2,3},{3,2},{4,5},{5,4},{6,7},{7,6},{8,9},{9,8},{10,11... | collective-permute-start | bytes 245768 | tf_op jit(solution)/shard_map/ppermute | solution.py:374
  21.9 1.3 %collective-permute-start.10 = (bf16[64,640]{1,0:T(8,128)(2,1)S(1)}, bf16[64,640]{1,0:T(8,128)(2,1)S(1)}, u32[]{:S(2)}, u32[]{:S(2)}) collective-permute-start(bf16[64,640]{1,0:T(8,128)(2,1)S(1)} %collective-permute-done.1.refs_12_), channel_id=1, source_target_pairs={{0,1},{1,0},{2,3},{3,2},{4,5},{5,4},{6,7},{7,6},{8,9},{9,8},{10,11... | collective-permute-start | bytes 245768 | tf_op jit(solution)/shard_map/ppermute | solution.py:374
